TPU v7x, 128 devices: a whole 4x4x4 slice. The times are simulated.
128 devices in a mesh: lat: 8 (over x, core), lon: 16 (over z, y).
Axes of the slice: x: 4, y: 4, z: 4, core: 2. Of those that a mesh axis runs over, the one named last changes fastest.
Arguments:
- grid_inputs: bfloat16 [384, 1024, 2, 227], P('lat', 'lon'), may hold values from -6 to 6
- mesh_latents: bfloat16 [4096, 512], P(('lat', 'lon')), may hold values from -6 to 6
- g2m_edges: bfloat16 [16384, 512], P(('lat', 'lon')), may hold values from -6 to 6
- g2m_sender: int32 [16384], P(('lat', 'lon')), may hold values from 0 to 393215, as said below
- g2m_receiver: int32 [16384], P(('lat', 'lon')), may hold values from 0 to 31
- mesh_edges: bfloat16 [32768, 512], P(('lat', 'lon')), may hold values from -6 to 6
- mesh_sender: int32 [32768], P(('lat', 'lon')), may hold values from 0 to 4095, as said below
- mesh_receiver: int32 [32768], P(('lat', 'lon')), may hold values from 0 to 31
- embed_w1: bfloat16 [227, 512], replicated, may hold values from -0.375 to 0.375
- embed_b1: float32 [512], replicated, may hold values from -3 to 3
- embed_w2: bfloat16 [512, 512], replicated, may hold values from -0.25 to 0.25
- embed_gain: float32 [512], replicated, may hold values from 0.5 to 1.5
- enc_edge_w1: bfloat16 [3, 512, 512], replicated, may hold values from -0.15625 to 0.15625
- enc_edge_b1: float32 [512], replicated, may hold values from -3 to 3
- enc_edge_w2: bfloat16 [512, 512], replicated, may hold values from -0.25 to 0.25
- enc_edge_gain: float32 [512], replicated, may hold values from 0.5 to 1.5
- enc_node_w1: bfloat16 [2, 512, 512], replicated, may hold values from -0.1875 to 0.1875
- enc_node_b1: float32 [512], replicated, may hold values from -3 to 3
- enc_node_w2: bfloat16 [512, 512], replicated, may hold values from -0.25 to 0.25
- enc_node_gain: float32 [512], replicated, may hold values from 0.5 to 1.5
- proc_edge_w1: bfloat16 [2, 3, 512, 512], replicated, may hold values from -0.15625 to 0.15625
- proc_edge_b1: float32 [2, 512], replicated, may hold values from -3 to 3
- proc_edge_w2: bfloat16 [2, 512, 512], replicated, may hold values from -0.25 to 0.25
- proc_edge_gain: float32 [2, 512], replicated, may hold values from 0.5 to 1.5
- proc_node_w1: bfloat16 [2, 2, 512, 512], replicated, may hold values from -0.1875 to 0.1875
- proc_node_b1: float32 [2, 512], replicated, may hold values from -3 to 3
- proc_node_w2: bfloat16 [2, 512, 512], replicated, may hold values from -0.25 to 0.25
- proc_node_gain: float32 [2, 512], replicated, may hold values from 0.5 to 1.5
Outputs:
- mesh_out: bfloat16 [4096, 2, 512], P(('lat', 'lon'))
Inputs may be any that keep to these rules, and one draw needn't show every extreme that they name: `g2m_sender`: A grid id is row * 1024 + column. The edges of one device's block (128 rows; devices in mesh order, lat slowest) start at grid rows within 2 of that device's 48 rows (kept inside the grid) and at columns within 2 of its 64 columns, counted around the globe. `mesh_sender`: A mesh id is the owning device's index in mesh order (lat slowest) times 32 plus its row there. A device beside another is one whose lat index differs by at most one (no wrap) and whose lon index differs by at most one counted around. Among the senders named in one device's block of 256 edges, exactly 4 distinct ones belong to each device beside it; senders of devices not beside it come from exactly 16 such devices, exactly 1 distinct ones from each.
All inputs are finite; a program needn't handle non-finite values.
Results may differ from a plain program's by a relative error of at most 0.02.
Values may be sent and summed in bfloat16 or wider, within the bound.
A program may use at most 128 MiB of HBM per device.

v0:
```python
import jax
import jax.numpy as jnp
from jax import lax
from jax.sharding import PartitionSpec as P

HALO = 2
STEPS = 2
NEAR_CAP = 4


def padded(cells, sides, width, closed):
    for axis, dim in sides:
        count = lax.axis_size(axis)
        ends = count if closed else count - 1
        head = lax.slice_in_dim(cells, 0, width, axis=dim)
        tail = lax.slice_in_dim(cells, cells.shape[dim] - width, cells.shape[dim], axis=dim)
        cells = jnp.concatenate(
            [
                lax.ppermute(tail, axis, [(i, (i + 1) % count) for i in range(ends)]),
                cells,
                lax.ppermute(head, axis, [((i + 1) % count, i) for i in range(ends)]),
            ],
            axis=dim,
        )
    return cells


def layer_norm(values, gain_vector):
    row_mean = jnp.mean(values, axis=-1, keepdims=True)
    centered = values - row_mean
    variance = jnp.mean(centered * centered, axis=-1, keepdims=True)
    return centered * lax.rsqrt(variance + 1e-05) * gain_vector


def embed_grid(inputs, embed_w1, embed_b1, embed_w2, embed_gain, send_weight):
    hidden = jax.nn.silu(
        jnp.dot(inputs, embed_w1, preferred_element_type=jnp.float32) + embed_b1
    ).astype(jnp.bfloat16)
    latent = layer_norm(
        jnp.dot(hidden, embed_w2, preferred_element_type=jnp.float32), embed_gain
    ).astype(jnp.bfloat16)
    return jnp.dot(latent, send_weight, preferred_element_type=jnp.float32).astype(jnp.bfloat16)


def edge_update(
    edge_rows, first_weight, senders, receivers, bias_vector, second_weight, gain_vector
):
    preact = jnp.dot(edge_rows, first_weight, preferred_element_type=jnp.float32)
    preact = preact + senders.astype(jnp.float32) + receivers.astype(jnp.float32) + bias_vector
    hidden = jax.nn.silu(preact).astype(jnp.bfloat16)
    update = layer_norm(
        jnp.dot(hidden, second_weight, preferred_element_type=jnp.float32), gain_vector
    )
    return (edge_rows.astype(jnp.float32) + update).astype(jnp.bfloat16)


def node_update(state_rows, summed, first_weights, bias_vector, second_weight, gain_vector):
    preact = jnp.dot(state_rows, first_weights[0], preferred_element_type=jnp.float32)
    preact = (
        preact + jnp.dot(summed, first_weights[1], preferred_element_type=jnp.float32) + bias_vector
    )
    hidden = jax.nn.silu(preact).astype(jnp.bfloat16)
    update = layer_norm(
        jnp.dot(hidden, second_weight, preferred_element_type=jnp.float32), gain_vector
    )
    return (state_rows.astype(jnp.float32) + update).astype(jnp.bfloat16)


def aggregate(selector, edge_rows):
    summed = jnp.dot(
        selector, edge_rows.reshape(edge_rows.shape[0], -1), preferred_element_type=jnp.float32
    )
    return summed.reshape(selector.shape[0], edge_rows.shape[1], edge_rows.shape[2]).astype(
        jnp.bfloat16
    )


def slot_picker(asked_rows, asked_slot, slot_count):
    slot_range = jnp.arange(slot_count, dtype=jnp.int32)
    chosen = (asked_slot[..., None, :] == slot_range[:, None]) & (asked_rows[..., None, :] == 1)
    return chosen.astype(jnp.bfloat16)


def on_device(
    grid_inputs,
    mesh_latents,
    g2m_edges,
    g2m_sender,
    g2m_receiver,
    mesh_edges,
    mesh_sender,
    mesh_receiver,
    embed_w1,
    embed_b1,
    embed_w2,
    embed_gain,
    enc_edge_w1,
    enc_edge_b1,
    enc_edge_w2,
    enc_edge_gain,
    enc_node_w1,
    enc_node_b1,
    enc_node_w2,
    enc_node_gain,
    proc_edge_w1,
    proc_edge_b1,
    proc_edge_w2,
    proc_edge_gain,
    proc_node_w1,
    proc_node_b1,
    proc_node_w2,
    proc_node_gain,
):
    lat_index = lax.axis_index("lat")
    lon_index = lax.axis_index("lon")
    lat_count = lax.axis_size("lat")
    lon_count = lax.axis_size("lon")
    devices = lat_count * lon_count
    own_device = lat_index * lon_count + lon_index
    lat_rows = grid_inputs.shape[0]
    lon_cols = grid_inputs.shape[1]
    mesh_rows = mesh_latents.shape[0]
    grid_send = embed_grid(grid_inputs, embed_w1, embed_b1, embed_w2, embed_gain, enc_edge_w1[1])
    lat_extended = padded(grid_send, (("lat", 0),), HALO, False)
    extended = padded(lat_extended, (("lon", 1),), HALO, True)
    ext_cols = extended.shape[1]
    grid_table = extended.reshape(
        extended.shape[0] * ext_cols, extended.shape[2], extended.shape[3]
    )
    grid_width = lon_cols * lon_count
    row_offset = g2m_sender // grid_width - lat_index * lat_rows + HALO
    col_offset = jnp.remainder(g2m_sender % grid_width - lon_index * lon_cols + HALO, grid_width)
    grid_senders = grid_table[row_offset * ext_cols + col_offset]
    mesh_recv = jnp.dot(mesh_latents, enc_edge_w1[2], preferred_element_type=jnp.float32).astype(
        jnp.bfloat16
    )
    g2m_new = edge_update(
        g2m_edges[:, None, :],
        enc_edge_w1[0],
        grid_senders,
        mesh_recv[g2m_receiver][:, None, :],
        enc_edge_b1,
        enc_edge_w2,
        enc_edge_gain,
    )
    node_range = jnp.arange(mesh_rows, dtype=jnp.int32)
    g2m_select = (g2m_receiver[None, :] == node_range[:, None]).astype(jnp.bfloat16)
    mesh_state = node_update(
        mesh_latents[:, None, :],
        aggregate(g2m_select, g2m_new),
        enc_node_w1,
        enc_node_b1,
        enc_node_w2,
        enc_node_gain,
    )
    owners = mesh_sender // mesh_rows
    local_rows = mesh_sender % mesh_rows
    remote = owners != own_device
    needed = (
        jnp.zeros((devices, mesh_rows), jnp.int32)
        .at[owners, local_rows]
        .max(remote.astype(jnp.int32))
    )
    slot_table = jnp.cumsum(needed, axis=1) - 1
    edge_rank = slot_table[owners, local_rows]
    asked_rows = lax.all_to_all(needed, ("lat", "lon"), split_axis=0, concat_axis=0, tiled=True)
    asked_slot = jnp.cumsum(asked_rows, axis=1) - 1
    near_count = NEAR_CAP
    edge_slot = jnp.where(
        remote, owners * near_count + edge_rank, devices * near_count + local_rows
    )
    picker = slot_picker(asked_rows, asked_slot, near_count)
    mesh_select = (mesh_receiver[None, :] == node_range[:, None]).astype(jnp.bfloat16)
    batch = mesh_state.shape[1]
    width = mesh_state.shape[2]
    edge_state = mesh_edges[:, None, :]
    for layer_index in range(STEPS):
        outgoing_proj = jnp.dot(
            mesh_state, proc_edge_w1[layer_index, 1], preferred_element_type=jnp.float32
        ).astype(jnp.bfloat16)
        incoming_proj = jnp.dot(
            mesh_state, proc_edge_w1[layer_index, 2], preferred_element_type=jnp.float32
        ).astype(jnp.bfloat16)
        outgoing = jnp.einsum(
            "dsr,rbh->dsbh", picker, outgoing_proj, preferred_element_type=jnp.float32
        ).astype(jnp.bfloat16)
        arrived = lax.all_to_all(outgoing, ("lat", "lon"), split_axis=0, concat_axis=0, tiled=True)
        sender_table = jnp.concatenate(
            [arrived.reshape(devices * near_count, batch, width), outgoing_proj], axis=0
        )
        edge_state = edge_update(
            edge_state,
            proc_edge_w1[layer_index, 0],
            sender_table[edge_slot],
            incoming_proj[mesh_receiver],
            proc_edge_b1[layer_index],
            proc_edge_w2[layer_index],
            proc_edge_gain[layer_index],
        )
        mesh_state = node_update(
            mesh_state,
            aggregate(mesh_select, edge_state),
            proc_node_w1[layer_index],
            proc_node_b1[layer_index],
            proc_node_w2[layer_index],
            proc_node_gain[layer_index],
        )
    return mesh_state


def solution(mesh):
    placed = (
        P("lat", "lon", None, None),
        P(("lat", "lon"), None),
        P(("lat", "lon"), None),
        P(("lat", "lon")),
        P(("lat", "lon")),
        P(("lat", "lon"), None),
        P(("lat", "lon")),
        P(("lat", "lon")),
        P(),
        P(),
        P(),
        P(),
        P(),
        P(),
        P(),
        P(),
        P(),
        P(),
        P(),
        P(),
        P(),
        P(),
        P(),
        P(),
        P(),
        P(),
        P(),
        P(),
    )
    return jax.shard_map(
        on_device,
        mesh=mesh,
        in_specs=placed,
        out_specs=P(("lat", "lon"), None, None),
        check_vma=False,
    )
```

profile of v0, /device:TPU:1, one launch (start us, length us, event | category | flops | bytes accessed | tf_op | source)
XLA Modules:
  0.0 187.7 jit_solution(17529681893109604386)
XLA Ops:
  1.0 10.9 %fusion.143 = (f32[48,64,2]{1,2,0:T(2,128)S(1)}, f32[48,64,2,512]{3,1,2,0:T(8,128)}) fusion(bf16[512,512]{1,0:T(8,128)(2,1)S(1)} %copy-done, f32[512]{0:T(512)} %param.37, bf16[48,64,2,227]{3,2,1,0:T(2,128)(2,1)} %param.28, bf16[227,512]{1,0:T(8,128)(2,1)} %param.36), kind=kOutput, calls=%fused_computation.210 | convolution fusion | flops 4671399936 | bytes 16155648 | tf_op jit(solution)/shard_map/dot_general | solution.py:40
  12.0 7.4 %multiply_reduce_fusion = f32[48,64,2]{1,2,0:T(2,128)S(1)} fusion(f32[48,64,2,512]{3,1,2,0:T(8,128)} %get-tuple-element.22, f32[48,64,2]{1,2,0:T(2,128)S(1)} %broadcast_multiply_fusion), kind=kLoop, calls=%fused_computation.9 | loop fusion | flops 9431040 | bytes 12632064 | tf_op jit(solution)/shard_map/reduce_sum | solution.py:31
  20.3 5.4 %fusion.7 = bf16[48,64,2,512]{3,1,2,0:T(8,128)(2,1)S(1)} fusion(f32[48,64,2,512]{3,1,2,0:T(8,128)S(1)} %copy-done.3, f32[512]{0:T(512)S(1)} %copy-done.39, f32[48,64,2]{1,2,0:T(2,128)S(1)} %add_rsqrt_fusion, f32[48,64,2]{1,2,0:T(2,128)S(1)} %broadcast_multiply_fusion, bf16[3,512,512]{2,1,0:T(8,128)(2,1)} %param.40), kind=kOutput, calls=%fused_computation.18 | convolution fusion | flops 3236954112 | bytes 19449856 | tf_op jit(solution)/shard_map/dot_general | solution.py:42
  25.8 2.7 %copy-done.2 = bf16[48,64,2,512]{3,1,2,0:T(8,128)(2,1)} copy-done((bf16[48,64,2,512]{3,1,2,0:T(8,128)(2,1)}, bf16[48,64,2,512]{3,1,2,0:T(8,128)(2,1)S(1)}, u32[]{:S(2)}) %copy-start.2) | copy-done | bytes 6291480
  28.5 4.6 %collective-permute-start = (bf16[2,64,2,512]{3,1,2,0:T(8,128)(2,1)S(1)}, bf16[2,64,2,512]{3,1,2,0:T(8,128)(2,1)S(1)}, u32[]{:S(2)}, u32[]{:S(2)}) collective-permute-start(bf16[2,64,2,512]{3,1,2,0:T(8,128)(2,1)S(1)} %get-tuple-element.9), channel_id=1, source_target_pairs={{0,16},{16,32},{32,48},{48,64},{64,80},{80,96},{96,112},{1,17},{17... | collective-permute-start | bytes 786440 | tf_op jit(solution)/shard_map/ppermute | solution.py:19
  33.1 1.9 %collective-permute-start.1 = (bf16[2,64,2,512]{3,1,2,0:T(8,128)(2,1)S(1)}, bf16[2,64,2,512]{3,1,2,0:T(8,128)(2,1)S(1)}, u32[]{:S(2)}, u32[]{:S(2)}) collective-permute-start(bf16[2,64,2,512]{3,1,2,0:T(8,128)(2,1)S(1)} %get-tuple-element.10), channel_id=1, source_target_pairs={{16,0},{32,16},{48,32},{64,48},{80,64},{96,80},{112,96},{17,1},{33... | collective-permute-start | bytes 786440 | tf_op jit(solution)/shard_map/ppermute | solution.py:21
  35.2 12.6 %scatter_fusion = s32[128,32]{0,1:T(8,128)S(1)} fusion(s32[128,32]{0,1:T(8,128)S(1)} %broadcast_in_dim.16, s32[256]{0:T(256)S(1)} %bitcast.212, s32[256]{0:T(256)S(1)} %get-tuple-element.5), kind=kCustom, calls=%fused_computation.7 | custom fusion | flops 256 | bytes 5120 | tf_op jit(solution)/shard_map/scatter-max | solution.py:162
  48.4 10.7 %all-to-all-start = ((s32[128,1,32]{2,1,0:T(1,128)}), s32[128,1,32]{2,1,0:T(1,128)S(1)}, u32[]{:S(2)}, u32[]{:S(2)}) async-start(s32[128,1,32]{2,1,0:T(1,128)} %copy.94), calls=%async_computation | async-start | bytes 131072 | tf_op jit(solution)/shard_map/all_to_all | solution.py:166
  59.3 1.2 convolution_convert_fusion.9
  60.5 1.3 fusion.51
  61.8 1.2 fusion.53
  63.0 2.0 %gather_fusion.2 = s32[256]{0:T(256)S(1)} fusion(s32[128,32]{0,1:T(8,128)S(1)} %broadcast_add_fusion, s32[256]{0:T(256)S(1)} %bitcast.213), kind=kCustom, calls=%fused_computation.2 | custom fusion | bytes 4096 | tf_op jit(solution)/shard_map/gather | solution.py:165
  69.1 1.7 pad_maximum_fusion.5
  70.8 1.1 collective-permute-start.2
  71.9 4.4 %collective-permute-start.3 = (bf16[52,2,2,512]{3,1,2,0:T(2,128)(2,1)S(1)}, bf16[52,2,2,512]{3,1,2,0:T(2,128)(2,1)S(1)}, u32[]{:S(2)}, u32[]{:S(2)}) collective-permute-start(bf16[52,2,2,512]{3,1,2,0:T(2,128)(2,1)S(1)} %get-tuple-element.8), channel_id=1, source_target_pairs={{1,0},{2,1},{3,2},{4,3},{5,4},{6,5},{7,6},{8,7},{9,8},{10,9},{11,1... | collective-permute-start | bytes 638984 | tf_op jit(solution)/shard_map/ppermute | solution.py:21
  76.3 4.7 %collective-permute-done.2 = bf16[52,2,2,512]{3,1,2,0:T(2,128)(2,1)S(1)} collective-permute-done((bf16[52,2,2,512]{3,1,2,0:T(2,128)(2,1)S(1)}, bf16[52,2,2,512]{3,1,2,0:T(2,128)(2,1)S(1)}, u32[]{:S(2)}, u32[]{:S(2)}) %collective-permute-start.2) | collective-permute-done | bytes 213024 | tf_op jit(solution)/shard_map/ppermute | solution.py:19
  81.1 6.8 %pad_maximum_fusion = bf16[52,68,2,512]{3,1,2,0:T(8,128)(2,1)S(1)} fusion(bf16[52,2,2,512]{3,1,2,0:T(2,128)(2,1)S(1)} %collective-permute-done.3, bf16[2,64,2,512]{3,1,2,0:T(8,128)(2,1)S(1)} %collective-permute-done.1, bf16[48,64,2,512]{3,1,2,0:T(8,128)(2,1)} %copy-done.2, bf16[2,64,2,512]{3,1,2,0:T(8,128)(2,1)S(1)} %collective-permute-done, ...), kind=kLoop, calls=%fused_computation.11 | loop fusion | flops 36208640 | bytes 14483456 | tf_op jit(solution)/shard_map/concatenate | solution.py:17
  87.9 4.9 %copy.91 = bf16[52,68,2,512]{3,2,1,0:T(2,128)(2,1)} copy(bf16[52,68,2,512]{3,1,2,0:T(8,128)(2,1)S(1)} %pad_maximum_fusion) | data formatting | bytes 14483456 | tf_op jit(solution)/shard_map/concatenate | solution.py:17
  92.8 4.2 %gather_fusion = bf16[128,2,512]{2,1,0:T(2,128)(2,1)S(1)} fusion(bf16[3536,2,512]{2,1,0:T(2,128)(2,1)} %bitcast.214, s32[1024]{0:T(1024)S(1)} %pad_clamp_fusion.3), kind=kCustom, calls=%fused_computation | custom fusion | bytes 524800 | tf_op jit(solution)/shard_map/gather | solution.py:133
  97.1 1.5 fusion.148
  99.2 1.4 multiply_convert_fusion.13
  102.1 1.2 convolution_convert_fusion.7
  103.9 2.1 %copy.97 = bf16[128,4,2,512]{3,2,1,0:T(2,128)(2,1)} copy(bf16[128,4,2,512]{3,0,2,1:T(8,128)(2,1)S(1)} %convolution_convert_fusion.1) | data formatting | bytes 2097152 | tf_op jit(solution)/shard_map/convert_element_type | solution.py:186
  106.0 9.8 %all-to-all-start.1 = ((bf16[128,4,2,512]{3,2,1,0:T(2,128)(2,1)}), bf16[128,4,2,512]{3,2,1,0:T(2,128)(2,1)S(1)}, u32[]{:S(2)}, u32[]{:S(2)}) async-start(bf16[128,4,2,512]{3,2,1,0:T(2,128)(2,1)} %copy.97), calls=%async_computation.1 | async-start | bytes 2097152 | tf_op jit(solution)/shard_map/all_to_all | solution.py:187
  116.4 2.2 %fusion.43 = f32[256,512]{1,0:T(8,128)} fusion(bf16[256,512]{1,0:T(8,128)(2,1)S(1)} %copy-done.5, bf16[2,3,512,512]{3,2,1,0:T(8,128)(2,1)} %param.48), kind=kOutput, calls=%fused_computation.72 | convolution fusion | flops 134217728 | bytes 1310720 | tf_op jit(solution)/shard_map/dot_general | solution.py:48
  118.7 1.2 convolution_convert_fusion.6
  120.0 2.5 %gather_fusion.4 = bf16[256,2,512]{2,1,0:T(2,128)(2,1)} fusion(bf16[32,2,512]{2,1,0:T(2,128)(2,1)S(1)} %copy.100, s32[1024]{0:T(1024)S(1)} %pad_clamp_fusion), kind=kCustom, calls=%fused_computation.4 | custom fusion | bytes 1049600 | tf_op jit(solution)/shard_map/gather | solution.py:195
  122.5 1.2 fusion.32
  123.8 10.8 %all-to-all-done.1 = bf16[128,4,2,512]{3,2,1,0:T(2,128)(2,1)S(1)} async-done(((bf16[128,4,2,512]{3,2,1,0:T(2,128)(2,1)}), bf16[128,4,2,512]{3,2,1,0:T(2,128)(2,1)S(1)}, u32[]{:S(2)}, u32[]{:S(2)}) %all-to-all-start.1) | async-done | bytes 1048608 | tf_op jit(solution)/shard_map/all_to_all | solution.py:187
  134.6 1.4 pad_maximum_fusion.1
  136.1 1.9 %gather_fusion.3 = bf16[256,2,512]{2,1,0:T(2,128)(2,1)S(1)} fusion(bf16[544,2,512]{2,1,0:T(2,128)(2,1)S(1)} %pad_maximum_fusion.1, s32[1024]{0:T(1024)} %pad_clamp_fusion.1), kind=kCustom, calls=%fused_computation.3 | custom fusion | bytes 1049600 | tf_op jit(solution)/shard_map/gather | solution.py:194
  138.0 1.9 %fusion.150 = (f32[256,2]{0,1:T(2,128)S(1)}, f32[256,2,512]{2,0,1:T(8,128)S(1)}) fusion(bf16[2,512,512]{2,1,0:T(8,128)(2,1)} %param.50, bf16[256,2,512]{2,1,0:T(2,128)(2,1)} %gather_fusion.4, bf16[256,2,512]{2,1,0:T(2,128)(2,1)S(1)} %gather_fusion.3, f32[512]{0:T(512)} %bitcast.228, f32[256,512]{1,0:T(8,128)} %fusion.43), kind=kOutput, calls=%fused_computation.213 | convolution fusion | flops 271318528 | bytes 3149824 | tf_op jit(solution)/shard_map/dot_general | solution.py:52
  141.4 1.5 multiply_convert_fusion.12
  142.9 1.3 fusion.151
  144.6 1.2 convolution_convert_fusion.4
  146.3 2.1 %copy.103 = bf16[128,4,2,512]{3,2,1,0:T(2,128)(2,1)} copy(bf16[128,4,2,512]{3,0,2,1:T(8,128)(2,1)S(1)} %convolution_convert_fusion) | data formatting | bytes 2097152 | tf_op jit(solution)/shard_map/convert_element_type | solution.py:186
  148.4 4.7 %all-to-all-start.2 = ((bf16[128,4,2,512]{3,2,1,0:T(2,128)(2,1)}), bf16[128,4,2,512]{3,2,1,0:T(2,128)(2,1)S(1)}, u32[]{:S(2)}, u32[]{:S(2)}) async-start(bf16[128,4,2,512]{3,2,1,0:T(2,128)(2,1)} %copy.103), calls=%async_computation.2 | async-start | bytes 2097152 | tf_op jit(solution)/shard_map/all_to_all | solution.py:187
  153.2 1.2 convolution_convert_fusion.3
  154.5 2.7 %gather_fusion.6 = bf16[256,2,512]{2,1,0:T(2,128)(2,1)} fusion(bf16[32,2,512]{2,1,0:T(2,128)(2,1)S(1)} %copy.106, s32[1024]{0:T(1024)} %copy-done.20), kind=kCustom, calls=%fused_computation.6 | custom fusion | bytes 1049600 | tf_op jit(solution)/shard_map/gather | solution.py:195
  157.2 1.2 fusion.25
  158.4 13.6 %all-to-all-done.2 = bf16[128,4,2,512]{3,2,1,0:T(2,128)(2,1)S(1)} async-done(((bf16[128,4,2,512]{3,2,1,0:T(2,128)(2,1)}), bf16[128,4,2,512]{3,2,1,0:T(2,128)(2,1)S(1)}, u32[]{:S(2)}, u32[]{:S(2)}) %all-to-all-start.2) | async-done | bytes 1048608 | tf_op jit(solution)/shard_map/all_to_all | solution.py:187
  172.1 2.4 %pad_maximum_fusion.2 = bf16[544,2,512]{2,1,0:T(2,128)(2,1)} fusion(bf16[32,2,512]{2,1,0:T(2,128)(2,1)S(1)} %copy.104, bf16[512,2,512]{2,1,0:T(2,128)(2,1)S(1)} %bitcast.216), kind=kLoop, calls=%fused_computation.40 | loop fusion | flops 557056 | bytes 2228224 | tf_op jit(solution)/shard_map/concatenate | solution.py:188
  174.5 3.9 %gather_fusion.5 = bf16[256,2,512]{2,1,0:T(2,128)(2,1)} fusion(bf16[544,2,512]{2,1,0:T(2,128)(2,1)} %pad_maximum_fusion.2, s32[1024]{0:T(1024)} %pad_clamp_fusion.1), kind=kCustom, calls=%fused_computation.5 | custom fusion | bytes 1049600 | tf_op jit(solution)/shard_map/gather | solution.py:194
  178.4 2.7 %fusion.152 = (f32[256,2]{0,1:T(2,128)S(1)}, f32[256,2,512]{2,0,1:T(8,128)S(1)}) fusion(bf16[2,512,512]{2,1,0:T(8,128)(2,1)} %param.50, bf16[256,2,512]{2,0,1:T(8,128)(2,1)} %copy-done.4, bf16[256,2,512]{2,1,0:T(2,128)(2,1)} %gather_fusion.6, bf16[256,2,512]{2,1,0:T(2,128)(2,1)} %gather_fusion.5, f32[512]{0:T(512)S(1)} %bitcast.226, ...), kind=kOutput, calls=%fused_computation.215 | convolution fusion | flops 539753984 | bytes 3674112 | tf_op jit(solution)/shard_map/dot_general | solution.py:52
  181.5 1.2 add_convert_fusion
  182.6 1.2 copy.108
  183.9 1.5 multiply_convert_fusion.11
  185.4 1.3 fusion.155
  (155 shorter events, 13.8 us)
Async XLA Ops:
  0.0 1.0 copy-start
  12.0 8.3 %copy-start.3 = (f32[48,64,2,512]{3,1,2,0:T(8,128)S(1)}, f32[48,64,2,512]{3,1,2,0:T(8,128)}, u32[]{:S(2)}) copy-start(f32[48,64,2,512]{3,1,2,0:T(8,128)} %get-tuple-element.22) | copy-start | bytes 37748740
  12.0 8.3 %copy-start.39 = (f32[512]{0:T(512)S(1)}, f32[512]{0:T(512)}, u32[]{:S(2)}) copy-start(f32[512]{0:T(512)} %param.39) | copy-start | bytes 6148
  20.3 14.8 %copy-start.21 = (s32[256]{0:T(256)S(1)}, s32[256]{0:T(256)}, u32[]{:S(2)}) copy-start(s32[256]{0:T(256)} %param.34) | copy-start | bytes 3076
  20.3 38.9 %copy-start.38 = (s32[128]{0:T(128)S(1)}, s32[128]{0:T(128)}, u32[]{:S(2)}) copy-start(s32[128]{0:T(128)} %param.31) | copy-start | bytes 1540
  20.3 38.9 %copy-start.8 = (bf16[32,512]{1,0:T(8,128)(2,1)S(1)}, bf16[32,512]{1,0:T(8,128)(2,1)}, u32[]{:S(2)}) copy-start(bf16[32,512]{1,0:T(8,128)(2,1)} %param.29) | copy-start | bytes 98308
  20.3 40.2 %copy-start.42 = (s32[128]{0:T(128)S(1)}, s32[128]{0:T(128)}, u32[]{:S(2)}) copy-start(s32[128]{0:T(128)} %param.32) | copy-start | bytes 1540
  20.3 40.2 %copy-start.6 = (bf16[128,512]{1,0:T(8,128)(2,1)S(1)}, bf16[128,512]{1,0:T(8,128)(2,1)}, u32[]{:S(2)}) copy-start(bf16[128,512]{1,0:T(8,128)(2,1)} %param.30) | copy-start | bytes 393220
  25.8 2.7 %copy-start.2 = (bf16[48,64,2,512]{3,1,2,0:T(8,128)(2,1)}, bf16[48,64,2,512]{3,1,2,0:T(8,128)(2,1)S(1)}, u32[]{:S(2)}) copy-start(bf16[48,64,2,512]{3,1,2,0:T(8,128)(2,1)S(1)} %fusion.7) | copy-start | bytes 18874372
  28.4 36.6 %copy-start.35 = (s32[256]{0:T(256)S(1)}, s32[256]{0:T(256)}, u32[]{:S(2)}) copy-start(s32[256]{0:T(256)} %param.35) | copy-start | bytes 3076
  28.4 36.6 %copy-start.27 = (f32[2,512]{1,0:T(2,128)S(1)}, f32[2,512]{1,0:T(2,128)}, u32[]{:S(2)}) copy-start(f32[2,512]{1,0:T(2,128)} %param.49) | copy-start | bytes 12292
  28.5 37.2 %copy-start.28 = (f32[2,512]{1,0:T(2,128)S(1)}, f32[2,512]{1,0:T(2,128)}, u32[]{:S(2)}) copy-start(f32[2,512]{1,0:T(2,128)} %param.51) | copy-start | bytes 12292
  28.5 37.8 %copy-start.29 = (f32[2,512]{1,0:T(2,128)S(1)}, f32[2,512]{1,0:T(2,128)}, u32[]{:S(2)}) copy-start(f32[2,512]{1,0:T(2,128)} %param.53) | copy-start | bytes 12292
  28.5 39.9 %copy-start.5 = (bf16[256,512]{1,0:T(8,128)(2,1)S(1)}, bf16[256,512]{1,0:T(8,128)(2,1)}, u32[]{:S(2)}) copy-start(bf16[256,512]{1,0:T(8,128)(2,1)} %param.33) | copy-start | bytes 786436
  28.5 40.5 %collective-permute-start = (bf16[2,64,2,512]{3,1,2,0:T(8,128)(2,1)S(1)}, bf16[2,64,2,512]{3,1,2,0:T(8,128)(2,1)S(1)}, u32[]{:S(2)}, u32[]{:S(2)}) collective-permute-start(bf16[2,64,2,512]{3,1,2,0:T(8,128)(2,1)S(1)} %get-tuple-element.9), channel_id=1, source_target_pairs={{0,16},{16,32},{32,48},{48,64},{64,80},{80,96},{96,112},{1,17},{17... | collective-permute-start | bytes 786440 | tf_op jit(solution)/shard_map/ppermute | solution.py:19
  33.1 35.9 %collective-permute-start.1 = (bf16[2,64,2,512]{3,1,2,0:T(8,128)(2,1)S(1)}, bf16[2,64,2,512]{3,1,2,0:T(8,128)(2,1)S(1)}, u32[]{:S(2)}, u32[]{:S(2)}) collective-permute-start(bf16[2,64,2,512]{3,1,2,0:T(8,128)(2,1)S(1)} %get-tuple-element.10), channel_id=1, source_target_pairs={{16,0},{32,16},{48,32},{64,48},{80,64},{96,80},{112,96},{17,1},{33... | collective-permute-start | bytes 786440 | tf_op jit(solution)/shard_map/ppermute | solution.py:21
  48.4 20.4 %all-to-all-start = ((s32[128,1,32]{2,1,0:T(1,128)}), s32[128,1,32]{2,1,0:T(1,128)S(1)}, u32[]{:S(2)}, u32[]{:S(2)}) async-start(s32[128,1,32]{2,1,0:T(1,128)} %copy.94), calls=%async_computation | async-start | bytes 131072 | tf_op jit(solution)/shard_map/all_to_all | solution.py:166
  70.8 10.2 %collective-permute-start.2 = (bf16[52,2,2,512]{3,1,2,0:T(2,128)(2,1)S(1)}, bf16[52,2,2,512]{3,1,2,0:T(2,128)(2,1)S(1)}, u32[]{:S(2)}, u32[]{:S(2)}) collective-permute-start(bf16[52,2,2,512]{3,1,2,0:T(2,128)(2,1)S(1)} %get-tuple-element.7), channel_id=1, source_target_pairs={{0,1},{1,2},{2,3},{3,4},{4,5},{5,6},{6,7},{7,8},{8,9},{9,10},{10,1... | collective-permute-start | bytes 638984 | tf_op jit(solution)/shard_map/ppermute | solution.py:19
  71.9 9.2 %collective-permute-start.3 = (bf16[52,2,2,512]{3,1,2,0:T(2,128)(2,1)S(1)}, bf16[52,2,2,512]{3,1,2,0:T(2,128)(2,1)S(1)}, u32[]{:S(2)}, u32[]{:S(2)}) collective-permute-start(bf16[52,2,2,512]{3,1,2,0:T(2,128)(2,1)S(1)} %get-tuple-element.8), channel_id=1, source_target_pairs={{1,0},{2,1},{3,2},{4,3},{5,4},{6,5},{7,6},{8,7},{9,8},{10,9},{11,1... | collective-permute-start | bytes 638984 | tf_op jit(solution)/shard_map/ppermute | solution.py:21
  76.3 27.1 %copy-start.9 = (pred[128,32]{0,1:T(8,128)(4,1)}, pred[128,32]{0,1:T(8,128)(4,1)S(1)}, u32[]{:S(2)}) copy-start(pred[128,32]{0,1:T(8,128)(4,1)S(1)} %compare_bitcast_fusion) | copy-start | bytes 12292
  87.9 9.2 %copy-start.40 = (f32[512]{0:T(512)S(1)}, f32[512]{0:T(512)}, u32[]{:S(2)}) copy-start(f32[512]{0:T(512)} %param.41) | copy-start | bytes 6148
  87.9 10.9 %copy-start.31 = (f32[512]{0:T(512)S(1)}, f32[512]{0:T(512)}, u32[]{:S(2)}) copy-start(f32[512]{0:T(512)} %param.43) | copy-start | bytes 6148
  92.8 6.3 %copy-start.41 = (f32[512]{0:T(512)S(1)}, f32[512]{0:T(512)}, u32[]{:S(2)}) copy-start(f32[512]{0:T(512)} %param.45) | copy-start | bytes 6148
  92.8 7.8 %copy-start.7 = (bf16[512,512]{1,0:T(8,128)(2,1)S(1)}, bf16[512,512]{1,0:T(8,128)(2,1)}, u32[]{:S(2)}) copy-start(bf16[512,512]{1,0:T(8,128)(2,1)} %param.46) | copy-start | bytes 1572868
  92.8 9.2 %copy-start.22 = (f32[512]{0:T(512)S(1)}, f32[512]{0:T(512)}, u32[]{:S(2)}) copy-start(f32[512]{0:T(512)} %param.47) | copy-start | bytes 6148
  97.1 18.7 %copy-start.30 = (f32[2,512]{1,0:T(2,128)S(1)}, f32[2,512]{1,0:T(2,128)}, u32[]{:S(2)}) copy-start(f32[2,512]{1,0:T(2,128)} %param.55) | copy-start | bytes 12292
  106.0 28.7 %all-to-all-start.1 = ((bf16[128,4,2,512]{3,2,1,0:T(2,128)(2,1)}), bf16[128,4,2,512]{3,2,1,0:T(2,128)(2,1)S(1)}, u32[]{:S(2)}, u32[]{:S(2)}) async-start(bf16[128,4,2,512]{3,2,1,0:T(2,128)(2,1)} %copy.97), calls=%async_computation.1 | async-start | bytes 2097152 | tf_op jit(solution)/shard_map/all_to_all | solution.py:187
  115.8 18.8 %copy-start.20 = (s32[1024]{0:T(1024)}, s32[1024]{0:T(1024)S(1)}, u32[]{:S(2)}) copy-start(s32[1024]{0:T(1024)S(1)} %pad_clamp_fusion) | copy-start | bytes 12292
  138.0 3.4 %copy-start.34 = (f32[1,512]{1,0:T(1,128)S(1)}, f32[1,512]{1,0:T(1,128)}, u32[]{:S(2)}) copy-start(f32[1,512]{1,0:T(1,128)} %get-tuple-element.14) | copy-start | bytes 6148
  138.0 3.4 %copy-start.36 = (s32[256]{0:T(256)S(1)}, s32[256]{0:T(256)}, u32[]{:S(2)}) copy-start(s32[256]{0:T(256)} %param.35) | copy-start | bytes 3076
  138.0 6.4 %copy-start.17 = (f32[32,2]{0,1:T(2,128)S(1)}, f32[32,2]{0,1:T(2,128)}, u32[]{:S(2)}) copy-start(f32[32,2]{0,1:T(2,128)} %copy-done.16) | copy-start | bytes 772
  138.0 6.4 %copy-start.19 = (f32[32,2]{0,1:T(2,128)S(1)}, f32[32,2]{0,1:T(2,128)}, u32[]{:S(2)}) copy-start(f32[32,2]{0,1:T(2,128)} %copy-done.18) | copy-start | bytes 772
  138.0 6.4 %copy-start.23 = (f32[512]{0:T(512)S(1)}, f32[512]{0:T(512)}, u32[]{:S(2)}) copy-start(f32[512]{0:T(512)} %param.47) | copy-start | bytes 6148
  138.0 6.4 %copy-start.26 = (f32[1,512]{1,0:T(1,128)S(1)}, f32[1,512]{1,0:T(1,128)}, u32[]{:S(2)}) copy-start(f32[1,512]{1,0:T(1,128)} %get-tuple-element.12) | copy-start | bytes 6148
  138.0 7.8 %copy-start.10 = (pred[128,32]{0,1:T(8,128)(4,1)S(1)}, pred[128,32]{0,1:T(8,128)(4,1)}, u32[]{:S(2)}) copy-start(pred[128,32]{0,1:T(8,128)(4,1)} %copy-done.9) | copy-start | bytes 12292
  140.0 8.4 %copy-start.11 = (f32[256,2]{0,1:T(2,128)}, f32[256,2]{0,1:T(2,128)S(1)}, u32[]{:S(2)}) copy-start(f32[256,2]{0,1:T(2,128)S(1)} %broadcast_multiply_fusion.2) | copy-start | bytes 6148
  140.2 8.1 %copy-start.13 = (f32[256,2]{0,1:T(2,128)}, f32[256,2]{0,1:T(2,128)S(1)}, u32[]{:S(2)}) copy-start(f32[256,2]{0,1:T(2,128)S(1)} %add_rsqrt_fusion.2) | copy-start | bytes 6148
  141.2 12.0 %copy-start.4 = (bf16[256,2,512]{2,0,1:T(8,128)(2,1)}, bf16[256,2,512]{2,0,1:T(8,128)(2,1)S(1)}, u32[]{:S(2)}) copy-start(bf16[256,2,512]{2,0,1:T(8,128)(2,1)S(1)} %add_convert_fusion.1) | copy-start | bytes 1572868
  144.2 34.2 %copy-start.33 = (f32[1,512]{1,0:T(1,128)S(1)}, f32[1,512]{1,0:T(1,128)}, u32[]{:S(2)}) copy-start(f32[1,512]{1,0:T(1,128)} %get-tuple-element.17) | copy-start | bytes 6148
  148.4 23.7 %all-to-all-start.2 = ((bf16[128,4,2,512]{3,2,1,0:T(2,128)(2,1)}), bf16[128,4,2,512]{3,2,1,0:T(2,128)(2,1)S(1)}, u32[]{:S(2)}, u32[]{:S(2)}) async-start(bf16[128,4,2,512]{3,2,1,0:T(2,128)(2,1)} %copy.103), calls=%async_computation.2 | async-start | bytes 2097152 | tf_op jit(solution)/shard_map/all_to_all | solution.py:187
  174.5 6.9 %copy-start.12 = (f32[256,2]{0,1:T(2,128)S(1)}, f32[256,2]{0,1:T(2,128)}, u32[]{:S(2)}) copy-start(f32[256,2]{0,1:T(2,128)} %copy-done.11) | copy-start | bytes 6148
  174.5 6.9 %copy-start.14 = (f32[256,2]{0,1:T(2,128)S(1)}, f32[256,2]{0,1:T(2,128)}, u32[]{:S(2)}) copy-start(f32[256,2]{0,1:T(2,128)} %copy-done.13) | copy-start | bytes 6148
  174.5 6.9 %copy-start.15 = (f32[1,512]{1,0:T(1,128)S(1)}, f32[1,512]{1,0:T(1,128)}, u32[]{:S(2)}) copy-start(f32[1,512]{1,0:T(1,128)} %get-tuple-element.16) | copy-start | bytes 6148
  174.5 6.9 %copy-start.24 = (f32[1,512]{1,0:T(1,128)S(1)}, f32[1,512]{1,0:T(1,128)}, u32[]{:S(2)}) copy-start(f32[1,512]{1,0:T(1,128)} %get-tuple-element.15) | copy-start | bytes 6148
  178.4 5.4 %copy-start.32 = (f32[1,512]{1,0:T(1,128)S(1)}, f32[1,512]{1,0:T(1,128)}, u32[]{:S(2)}) copy-start(f32[1,512]{1,0:T(1,128)} %get-tuple-element.13) | copy-start | bytes 6148
  178.4 5.5 %copy-start.37 = (s32[256]{0:T(256)S(1)}, s32[256]{0:T(256)}, u32[]{:S(2)}) copy-start(s32[256]{0:T(256)} %param.35) | copy-start | bytes 3076
  178.4 8.5 %copy-start.25 = (f32[1,512]{1,0:T(1,128)S(1)}, f32[1,512]{1,0:T(1,128)}, u32[]{:S(2)}) copy-start(f32[1,512]{1,0:T(1,128)} %get-tuple-element.11) | copy-start | bytes 6148
  178.4 9.3 %copy-start.1 = (bf16[512,512]{1,0:T(8,128)(2,1)S(1)}, bf16[512,512]{1,0:T(8,128)(2,1)}, u32[]{:S(2)}) copy-start(bf16[512,512]{1,0:T(8,128)(2,1)} %param.38) | copy-start | bytes 1572868
  (2 other events, 1.1 us)
where the time goes:
time: 189 us; the launch traced here: 188 us
  matrix products  44 us (23%)
  local copies, waits for them, and re-layouts  38.6 us (20%)
  starting transfers between devices  37.3 us (20%)
  other arithmetic  37.2 us (20%)
  waiting for transfers between devices  29.6 us (16%)
    all_to_all x2, waiting for transfers between devices, on_device(): lax.all_to_all(outgoing, ('lat', 'lon'), split_axis=0, concat_axis=0, til...  24.5 us
    all_to_all x2, starting transfers between devices, on_device(): lax.all_to_all(outgoing, ('lat', 'lon'), split_axis=0, concat_axis=0, til...  14.6 us
    another operation x1, other arithmetic, on_device(): needed = jnp.zeros((devices, mesh_rows), jnp.int32).at[owners, local_rows...  12.6 us
    dot_general x1, matrix products, embed_grid(): jnp.dot(hidden, embed_w2, preferred_element_type=jnp.float32)  10.9 us
    all_to_all x1, starting transfers between devices, on_device(): lax.all_to_all(needed, ('lat', 'lon'), split_axis=0, concat_axis=0, tiled...  10.7 us
    reduce_sum x7, other arithmetic, layer_norm(): variance = jnp.mean(centered * centered, axis=-1, keepdims=True)  8.63 us
    concatenate x1, other arithmetic, padded(): jnp.concatenate([lax.ppermute(tail, axis, [(i, (i + 1) % count) for i in...  6.79 us
    ppermute x2, starting transfers between devices, padded(): lax.ppermute(head, axis, [((i + 1) % count, i) for i in range(ends)])  6.36 us
  transfers between devices with their start and end apart: 7, of which 4 were waited for; matrix products, arithmetic and copies ran while one was open for 19% of the time, Pallas kernels for 0%

commit v1 on v0

v1 whole, which is shorter than its diff:
```python
from typing import Any, NamedTuple

import jax
import jax.numpy as jnp
from jax import lax
from jax.experimental import pallas as pl
from jax.experimental.pallas import tpu as pltpu
from jax.sharding import PartitionSpec as P

BF = jnp.bfloat16
F32 = jnp.float32
I32 = jnp.int32
MESH = pl.DeviceIdType.MESH

BATCH = 2
D = 512
HALO = 2
STEPS = 2
LATS = 8
LONS = 16
PAIRS = LATS * LONS
NODES = 32
GRID_EDGES = 128
EDGES = 256
NEAR = (1, 15, 16, 17, 31, 112, 113, 127)
EXTRA = 3
SLOTS = PAIRS + EXTRA * len(NEAR)
DIRECTIONS = tuple((a, b) for a in (0, -1, 1) for b in (0, -1, 1) if (a, b) != (0, 0))


class Given(NamedTuple):
    grid_inputs: Any
    mesh_latents: Any
    g2m_edges: Any
    g2m_sender: Any
    g2m_receiver: Any
    mesh_edges: Any
    mesh_sender: Any
    mesh_receiver: Any
    embed_w1: Any
    embed_b1: Any
    embed_w2: Any
    embed_gain: Any
    enc_edge_w1: Any
    enc_edge_b1: Any
    enc_edge_w2: Any
    enc_edge_gain: Any
    enc_node_w1: Any
    enc_node_b1: Any
    enc_node_w2: Any
    enc_node_gain: Any
    proc_edge_w1: Any
    proc_edge_b1: Any
    proc_edge_w2: Any
    proc_edge_gain: Any
    proc_node_w1: Any
    proc_node_b1: Any
    proc_node_w2: Any
    proc_node_gain: Any


class Held(NamedTuple):
    g2m_receiver: Any
    mesh_sender: Any
    mesh_receiver: Any
    mesh_latents: Any
    g2m_edges: Any
    enc_edge_w1: Any
    enc_edge_b1: Any
    embed_w1: Any
    embed_b1: Any
    embed_w2: Any
    embed_gain: Any
    enc_edge_w2: Any
    enc_edge_gain: Any
    enc_node_w1: Any
    enc_node_b1: Any
    enc_node_w2: Any
    enc_node_gain: Any
    mesh_edges: Any
    proc_edge_w1: Any
    proc_edge_b1: Any
    proc_edge_w2: Any
    proc_edge_gain: Any
    proc_node_w1: Any
    proc_node_b1: Any
    proc_node_w2: Any
    proc_node_gain: Any


FETCHED = len(Held._fields)


def mm(a, b):
    return jnp.dot(a, b, preferred_element_type=F32)


def mm_nt(a, b):
    return lax.dot_general(a, b, (((1,), (1,)), ((), ())), preferred_element_type=F32)


def iota(shape, dim):
    return lax.broadcasted_iota(I32, shape, dim)


def hot(mask):
    return jnp.where(mask, 1.0, 0.0).astype(BF)


def silu(v):
    half = 0.5 * v
    return half + half * jnp.tanh(half)


def norm(v, gain):
    centered = v - jnp.mean(v, axis=-1, keepdims=True)
    variance = jnp.mean(centered * centered, axis=-1, keepdims=True)
    return centered * lax.rsqrt(variance + 1e-05) * gain


def doubled_column(row, count):
    shape = (2 * count, count)
    spread = jnp.where(iota(shape, 1) == (iota(shape, 0) >> 1), row.astype(F32), 0.0)
    return jnp.sum(spread, axis=1, keepdims=True).astype(I32)


def doubled_row(row, count):
    shape = (count, 2 * count)
    return mm(row.astype(F32).astype(BF), hot((iota(shape, 1) >> 1) == iota(shape, 0))).astype(I32)


def kernel(*refs):
    grid_hbm, sender_hbm = refs[:2]
    hbm = refs[2 : 2 + FETCHED]
    out_ref = refs[2 + FETCHED]
    refs = refs[3 + FETCHED :]
    held = Held(*refs[:FETCHED])
    (
        cells, sender, picked, pick_all, gather_far, gather_own, gather_recv, edge_base,
        req_out, req_in, out_rows, in_rows,
        fetch_sem, cells_sem, sender_sem,
        halo_send, halo_recv, req_send, req_recv, row_send, row_recv,
    ) = refs[FETCHED:]

    lat = lax.axis_index("lat")
    lon = lax.axis_index("lon")
    lat_rows, lon_cols = grid_hbm.shape[:2]

    sender_copy = pltpu.make_async_copy(sender_hbm, sender, sender_sem)
    sender_copy.start()
    fetches = [
        pltpu.make_async_copy(hbm[n], held[n], fetch_sem.at[n]) for n in range(FETCHED)
    ]
    fetch = Held(*fetches)

    def ready(*copies):
        for copy in copies:
            copy.wait()

    for copy in fetches[:3]:
        copy.start()
    cells_copy = pltpu.make_async_copy(
        grid_hbm, cells.at[pl.ds(HALO, lat_rows), pl.ds(HALO, lon_cols)], cells_sem
    )
    cells_copy.start()
    for copy in fetches[3:]:
        copy.start()

    def place(step_lat, step_lon, sign):
        return (
            (lat + sign * step_lat + LATS) & (LATS - 1),
            (lon + sign * step_lon + LONS) & (LONS - 1),
        )

    def for_all_others(act):
        for step_lon in range(1, LONS):
            act(0, step_lon)

        def band(step_lat, carry):
            for step_lon in range(LONS):
                act(step_lat, step_lon)
            return carry

        lax.fori_loop(1, LATS, band, 0)

    barrier = pltpu.get_barrier_semaphore()

    def greet(step_lat, step_lon):
        pl.semaphore_signal(
            barrier, inc=1, device_id=place(step_lat, step_lon, 1), device_id_type=MESH
        )

    for_all_others(greet)

    ready(fetch.g2m_receiver, fetch.mesh_sender, fetch.mesh_receiver)
    senders = held.mesh_sender[...]
    owner = senders >> 5
    row = senders & (NODES - 1)
    rel = ((((owner >> 4) - lat) & (LATS - 1)) << 4) | (((owner & 15) - lon) & (LONS - 1))
    owner2 = hot((iota((2 * PAIRS, EDGES), 0) >> 1) == rel)
    row2 = hot((iota((128, EDGES), 0) >> 1) == row)
    asked = mm_nt(owner2, row2)
    shape = (2 * PAIRS, 128)
    same = (iota(shape, 0) & 1) == (iota(shape, 1) & 1)
    asked = hot((asked > 0.5) & same & (iota(shape, 0) >= 2))
    req_out[...] = asked.reshape(PAIRS, 2, 128)
    req_in[0] = jnp.zeros((2, 128), BF)
    for t in range(STEPS):
        in_rows[t, 0] = jnp.zeros((2, D), BF)

    pl.semaphore_wait(barrier, PAIRS - 1)

    spans = {0: (0, lat_rows, HALO), -1: (0, HALO, HALO + lat_rows), 1: (lat_rows - HALO, HALO, 0)}
    spans_lon = {
        0: (0, lon_cols, HALO), -1: (0, HALO, HALO + lon_cols), 1: (lon_cols - HALO, HALO, 0)
    }
    halo = []
    for n, (a, b) in enumerate(DIRECTIONS):
        row0, rows, to_row = spans[a]
        col0, cols, to_col = spans_lon[b]
        halo.append(
            pltpu.make_async_remote_copy(
                src_ref=grid_hbm.at[pl.ds(row0, rows), pl.ds(col0, cols)],
                dst_ref=cells.at[pl.ds(to_row, rows), pl.ds(to_col, cols)],
                send_sem=halo_send.at[n],
                recv_sem=halo_recv.at[n],
                device_id=((lat + a + LATS) & (LATS - 1), (lon + b + LONS) & (LONS - 1)),
                device_id_type=MESH,
            )
        )
    groups = [
        [copy for copy, (a, _) in zip(halo, DIRECTIONS) if a == which] for which in (0, -1, 1)
    ]
    has_before = lat > 0
    has_after = lat < LATS - 1

    for copy in groups[0]:
        copy.start()

    @pl.when(has_before)
    def _():
        for copy in groups[1]:
            copy.start()

    @pl.when(has_after)
    def _():
        for copy in groups[2]:
            copy.start()

    def ask(step_lat, step_lon):
        i = step_lat * LONS + step_lon
        pltpu.make_async_remote_copy(
            src_ref=req_out.at[i], dst_ref=req_in.at[i], send_sem=req_send, recv_sem=req_recv,
            device_id=place(step_lat, step_lon, 1), device_id_type=MESH,
        ).start()

    for_all_others(ask)

    owner1 = hot(iota((PAIRS, EDGES), 0) == rel)
    row1 = iota((NODES, EDGES), 0) == row
    needed = hot(mm_nt(hot(row1), owner1) > 0.5)
    below = hot(iota((NODES, NODES), 1) < iota((NODES, NODES), 0))
    order = mm(below, needed).astype(BF)
    rank = jnp.sum(jnp.where(row1, mm(order, owner1), 0.0), axis=0, keepdims=True).astype(I32)
    near = jnp.zeros_like(rel)
    for n, i in enumerate(NEAR):
        near = jnp.where(rel == i, n, near)
    slot = jnp.where(rank == 0, rel, PAIRS + EXTRA * near + rank - 1)
    slot = jnp.where(rel == 0, SLOTS + row, slot)
    slot_column = doubled_column(slot, EDGES)
    shape = (2 * EDGES, 2 * (SLOTS + NODES))
    gather = hot(iota(shape, 1) == 2 * slot_column + (iota(shape, 0) & 1))
    gather_far[...] = gather[:, : 2 * SLOTS]
    gather_own[...] = gather[:, 2 * SLOTS :]
    receivers = held.mesh_receiver[...]
    shape = (2 * EDGES, 2 * NODES)
    gather_recv[...] = hot(
        iota(shape, 1) == 2 * doubled_column(receivers, EDGES) + (iota(shape, 0) & 1)
    )
    shape = (2 * NODES, 2 * EDGES)
    total_mesh = hot(iota(shape, 0) == 2 * doubled_row(receivers, EDGES) + (iota(shape, 1) & 1))

    grid_receivers = held.g2m_receiver[...]
    shape = (2 * NODES, 2 * GRID_EDGES)
    total_grid = hot(
        iota(shape, 0) == 2 * doubled_row(grid_receivers, GRID_EDGES) + (iota(shape, 1) & 1)
    )
    shape = (2 * GRID_EDGES, NODES)
    gather_grid_recv = hot(iota(shape, 1) == doubled_column(grid_receivers, GRID_EDGES))

    ready(fetch.mesh_latents, fetch.g2m_edges, fetch.enc_edge_w1, fetch.enc_edge_b1)
    latents = held.mesh_latents[...]
    shape = (2 * GRID_EDGES, GRID_EDGES)
    grid_edges = mm(hot(iota(shape, 1) == (iota(shape, 0) >> 1)), held.g2m_edges[...]).astype(BF)
    mesh_recv = mm(latents, held.enc_edge_w1[2]).astype(BF)
    grid_base = (
        mm(grid_edges, held.enc_edge_w1[0])
        + mm(gather_grid_recv, mesh_recv)
        + held.enc_edge_b1[...]
    )
    shape = (2 * NODES, NODES)
    state = mm(hot(iota(shape, 1) == (iota(shape, 0) >> 1)), latents).astype(BF)
    ready(fetch.mesh_edges)
    shape = (2 * EDGES, EDGES)
    edge_state = mm(
        hot(iota(shape, 1) == (iota(shape, 0) >> 1)), held.mesh_edges[...]
    ).astype(BF)

    sender_copy.wait()
    cells_copy.wait()
    for copy in groups[0]:
        copy.wait_recv()

    @pl.when(has_after)
    def _():
        for copy in groups[1]:
            copy.wait_recv()

    @pl.when(has_before)
    def _():
        for copy in groups[2]:
            copy.wait_recv()

    width = lon_cols * LONS

    def pick(k, carry):
        cell = sender[k]
        cell_row = (cell // width) - lat * lat_rows + HALO
        cell_col = ((cell & (width - 1)) - lon * lon_cols + HALO + width) & (width - 1)
        cell_row = jnp.clip(cell_row, 0, cells.shape[0] - 1)
        cell_col = jnp.clip(cell_col, 0, cells.shape[1] - 1)
        picked[k] = cells[cell_row, cell_col]
        return carry

    lax.fori_loop(0, GRID_EDGES, pick, 0, unroll=8)

    ready(fetch.embed_w1, fetch.embed_b1, fetch.embed_w2, fetch.embed_gain)
    inputs = picked[...].reshape(2 * GRID_EDGES, picked.shape[2])
    hidden = silu(mm(inputs, held.embed_w1[...]) + held.embed_b1[...]).astype(BF)
    latent = norm(mm(hidden, held.embed_w2[...]), held.embed_gain[...]).astype(BF)
    preact = mm(latent, held.enc_edge_w1[1]) + grid_base
    hidden = silu(preact).astype(BF)
    ready(fetch.enc_edge_w2, fetch.enc_edge_gain)
    update = norm(mm(hidden, held.enc_edge_w2[...]), held.enc_edge_gain[...])
    new_edges = (grid_edges.astype(F32) + update).astype(BF)
    summed = mm(total_grid, new_edges).astype(BF)
    ready(fetch.enc_node_w1, fetch.enc_node_b1, fetch.enc_node_w2, fetch.enc_node_gain)
    preact = (
        mm(state, held.enc_node_w1[0])
        + mm(summed, held.enc_node_w1[1])
        + held.enc_node_b1[...]
    )
    hidden = silu(preact).astype(BF)
    update = norm(mm(hidden, held.enc_node_w2[...]), held.enc_node_gain[...])
    state = (state.astype(F32) + update).astype(BF)

    pltpu.make_async_copy(
        req_in.at[pl.ds(1, PAIRS - 1)], req_in.at[pl.ds(1, PAIRS - 1)], req_recv
    ).wait()
    wanted = req_in[...].reshape(2 * PAIRS, 128)[:, : 2 * NODES]
    shape = (2 * NODES, 2 * NODES)
    before = hot(
        (iota(shape, 0) < iota(shape, 1)) & ((iota(shape, 0) & 1) == (iota(shape, 1) & 1))
    )
    place_of = mm(wanted, before).astype(BF)
    first = jnp.where(place_of.astype(F32) < 0.5, wanted.astype(F32), 0.0).astype(BF)
    shape = (2 * EXTRA * len(NEAR), 2 * PAIRS)
    line = iota(shape, 0)
    which = jnp.zeros_like(line)
    target = jnp.full_like(line, NEAR[0])
    for n in range(1, len(NEAR)):
        later = line >= 2 * EXTRA * n
        which = jnp.where(later, n, which)
        target = jnp.where(later, NEAR[n], target)
    choose = hot(iota(shape, 1) == 2 * target + (line & 1))
    kth = ((line >> 1) - EXTRA * which + 1).astype(F32)[:, : 2 * NODES]
    more = jnp.where(mm(choose, place_of) == kth, mm(choose, wanted), 0.0).astype(BF)
    pick_all[: 2 * PAIRS] = first
    pick_all[2 * PAIRS :] = more

    ready(fetch.proc_edge_w1, fetch.proc_edge_b1, fetch.proc_edge_w2, fetch.proc_edge_gain)
    ready(fetch.proc_node_w1, fetch.proc_node_b1, fetch.proc_node_w2, fetch.proc_node_gain)
    for t in range(STEPS):
        outgoing = mm(state, held.proc_edge_w1[t, 1]).astype(BF)
        out_rows[t] = mm(pick_all[...], outgoing).astype(BF).reshape(SLOTS, 2, D)

        def give(step_lat, step_lon, t=t):
            i = step_lat * LONS + step_lon
            pltpu.make_async_remote_copy(
                src_ref=out_rows.at[t, i], dst_ref=in_rows.at[t, i],
                send_sem=row_send.at[t], recv_sem=row_recv.at[t],
                device_id=place(step_lat, step_lon, -1), device_id_type=MESH,
            ).start()

        for_all_others(give)
        for n, i in enumerate(NEAR):
            span = pl.ds(PAIRS + EXTRA * n, EXTRA)
            pltpu.make_async_remote_copy(
                src_ref=out_rows.at[t, span], dst_ref=in_rows.at[t, span],
                send_sem=row_send.at[t], recv_sem=row_recv.at[t],
                device_id=place(i // LONS, i % LONS, -1), device_id_type=MESH,
            ).start()

        incoming = mm(state, held.proc_edge_w1[t, 2]).astype(BF)
        edge_base[...] = (
            mm(edge_state, held.proc_edge_w1[t, 0])
            + mm(gather_recv[...], incoming)
            + mm(gather_own[...], outgoing)
            + held.proc_edge_b1[t : t + 1]
        )
        node_base = mm(state, held.proc_node_w1[t, 0]) + held.proc_node_b1[t : t + 1]

        arrived = in_rows.at[t, pl.ds(1, SLOTS - 1)]
        pltpu.make_async_copy(arrived, arrived, row_recv.at[t]).wait()
        table = in_rows[t].reshape(2 * SLOTS, D)
        hidden = silu(edge_base[...] + mm(gather_far[...], table)).astype(BF)
        update = norm(mm(hidden, held.proc_edge_w2[t]), held.proc_edge_gain[t : t + 1])
        edge_state = (edge_state.astype(F32) + update).astype(BF)
        summed = mm(total_mesh, edge_state).astype(BF)
        hidden = silu(node_base + mm(summed, held.proc_node_w1[t, 1])).astype(BF)
        update = norm(mm(hidden, held.proc_node_w2[t]), held.proc_node_gain[t : t + 1])
        state = (state.astype(F32) + update).astype(BF)

    out_ref[...] = state.reshape(NODES, 2, D)

    for copy in groups[0]:
        copy.wait_send()

    @pl.when(has_before)
    def _():
        for copy in groups[1]:
            copy.wait_send()

    @pl.when(has_after)
    def _():
        for copy in groups[2]:
            copy.wait_send()

    asked_all = req_out.at[pl.ds(1, PAIRS - 1)]
    pltpu.make_async_copy(asked_all, asked_all, req_send).wait()
    for t in range(STEPS):
        sent = out_rows.at[t, pl.ds(1, SLOTS - 1)]
        pltpu.make_async_copy(sent, sent, row_send.at[t]).wait()


def on_device(*args):
    given = Given(*args)
    lat_rows, lon_cols, batch, width = given.grid_inputs.shape

    def flat(row):
        return row.reshape(1, row.shape[0])

    wanted = Held(
        flat(given.g2m_receiver),
        flat(given.mesh_sender),
        flat(given.mesh_receiver),
        given.mesh_latents,
        given.g2m_edges,
        given.enc_edge_w1,
        flat(given.enc_edge_b1),
        given.embed_w1,
        flat(given.embed_b1),
        given.embed_w2,
        flat(given.embed_gain),
        given.enc_edge_w2,
        flat(given.enc_edge_gain),
        given.enc_node_w1,
        flat(given.enc_node_b1),
        given.enc_node_w2,
        flat(given.enc_node_gain),
        given.mesh_edges,
        given.proc_edge_w1,
        given.proc_edge_b1,
        given.proc_edge_w2,
        given.proc_edge_gain,
        given.proc_node_w1,
        given.proc_node_b1,
        given.proc_node_w2,
        given.proc_node_gain,
    )
    operands = [given.grid_inputs, given.g2m_sender, *wanted]
    dma = pltpu.SemaphoreType.DMA
    scratch = [pltpu.VMEM(part.shape, part.dtype) for part in wanted]
    scratch += [
        pltpu.VMEM((lat_rows + 2 * HALO, lon_cols + 2 * HALO, batch, width), BF),
        pltpu.SMEM((GRID_EDGES,), I32),
        pltpu.VMEM((GRID_EDGES, batch, width), BF),
        pltpu.VMEM((2 * SLOTS, 2 * NODES), BF),
        pltpu.VMEM((2 * EDGES, 2 * SLOTS), BF),
        pltpu.VMEM((2 * EDGES, 2 * NODES), BF),
        pltpu.VMEM((2 * EDGES, 2 * NODES), BF),
        pltpu.VMEM((2 * EDGES, D), F32),
        pltpu.VMEM((PAIRS, 2, 128), BF),
        pltpu.VMEM((PAIRS, 2, 128), BF),
        pltpu.VMEM((STEPS, SLOTS, 2, D), BF),
        pltpu.VMEM((STEPS, SLOTS, 2, D), BF),
        dma((FETCHED,)),
        dma,
        dma,
        dma((len(DIRECTIONS),)),
        dma((len(DIRECTIONS),)),
        dma,
        dma,
        dma((STEPS,)),
        dma((STEPS,)),
    ]
    return pl.pallas_call(
        kernel,
        out_shape=jax.ShapeDtypeStruct((NODES, batch, D), BF),
        in_specs=[pl.BlockSpec(memory_space=pl.ANY)] * len(operands),
        out_specs=pl.BlockSpec(memory_space=pltpu.VMEM),
        scratch_shapes=scratch,
        cost_estimate=pl.CostEstimate(
            flops=4 * 10**9, bytes_accessed=15 * 10**6, transcendentals=10**6
        ),
        compiler_params=pltpu.CompilerParams(
            collective_id=0, has_side_effects=True, vmem_limit_bytes=64 * 2**20
        ),
    )(*operands)


def solution(mesh):
    nodes = P(("lat", "lon"), None)
    edges = P(("lat", "lon"))
    split = [P("lat", "lon", None, None), nodes, nodes, edges, edges, nodes, edges, edges]
    split += [P()] * (len(Given._fields) - len(split))
    return jax.shard_map(
        on_device,
        mesh=mesh,
        in_specs=tuple(split),
        out_specs=P(("lat", "lon"), None, None),
        check_vma=False,
    )
```

time: 189 us -> 42.5 us (0.22)
  matrix products: 44 us -> 0 us
  Pallas kernels: 0 us -> 40.8 us
  starting transfers between devices: 37.3 us -> 0 us
  other arithmetic: 37.2 us -> 0 us
  local copies, waits for them, and re-layouts: 38.6 us -> 1.52 us
  waiting for transfers between devices: 29.6 us -> 0 us
    dot_general x23 -> x0, matrix products: 44 us -> none  [the longest x1 10.9 us: embed_grid(): jnp.dot(hidden, embed_w2, preferred_element_type=jnp.float32)]
    pallas_call x0 -> x1, Pallas kernels: none -> 40.8 us  [on_device(): pl.pallas_call(kernel, out_shape=jax.ShapeDtypeStruct((NODES, batch, D),...]
    all_to_all x3 -> x0, starting transfers between devices: 25.2 us -> none  [the longest x2 14.6 us: on_device(): lax.all_to_all(outgoing, ('lat', 'lon'), split_axis=0, concat_axis=0, til...]
    all_to_all x3 -> x0, waiting for transfers between devices: 24.9 us -> none  [the longest x2 24.5 us: on_device(): lax.all_to_all(outgoing, ('lat', 'lon'), split_axis=0, concat_axis=0, til...]
    gather x7 -> x0, local copies, waits for them, and re-layouts: 18 us -> none  [the longest x2 5.77 us: on_device(): sender_table[edge_slot]]
    another operation x3 -> x0, other arithmetic: 12.7 us -> none  [the longest x1 12.6 us: on_device(): needed = jnp.zeros((devices, mesh_rows), jnp.int32).at[owners, local_rows...]
    ppermute x4 -> x0, starting transfers between devices: 12 us -> none  [the longest x2 6.36 us: padded(): lax.ppermute(head, axis, [((i + 1) % count, i) for i in range(ends)])]
    concatenate x4 -> x0, other arithmetic: 10.7 us -> none  [the longest x1 6.79 us: padded(): jnp.concatenate([lax.ppermute(tail, axis, [(i, (i + 1) % count) for i in...]
  transfers between devices with their start and end apart: 7 -> 0, of which waited for: 4 -> 0; matrix products, arithmetic and copies ran while one was open for 19% -> 0% of each run, Pallas kernels for 0% -> 0%
where the time goes in v1:
time: 42.5 us; the launch traced here: 42.3 us
  Pallas kernels  40.8 us (96%)
  local copies, waits for them, and re-layouts  1.52 us (4%)
    pallas_call x1, Pallas kernels, on_device(): pl.pallas_call(kernel, out_shape=jax.ShapeDtypeStruct((NODES, batch, D),...  40.8 us
    unnamed x1, local copies, waits for them, and re-layouts  1.52 us

profile of v1, /device:TPU:1, one launch (start us, length us, event | category | flops | bytes accessed | tf_op | source)
XLA Modules:
  0.0 42.3 jit_solution(16196165282705469718)
XLA Ops:
  0.0 40.8 %shard_map.262 = bf16[32,2,512]{2,1,0:T(2,128)(2,1)} custom-call(bf16[48,64,2,227]{3,2,1,0:T(2,128)(2,1)} %refs_0_.1, s32[128]{0:T(128)} %refs_1_.1, s32[1,128]{1,0:T(1,128)} %bitcast.17, s32[1,256]{1,0:T(1,128)} %bitcast.15, s32[1,256]{1,0:T(1,128)} %bitcast.16, bf16[32,512]{1,0:T(8,128)(2,1)} %refs_5_.1, bf16[128,512]{1,0:T(8,128)(2,1)} %refs_6_.1, ...), custom_call_target="tpu_custom_call" | custom-call | flops 4000000000 | bytes 15000000 | tf_op jit(solution)/shard_map/pallas_call | solution.py:507
  40.8 1.5 %copy.30 = bf16[32,2,512]{2,1,0:T(2,128)(2,1)} copy(bf16[32,2,512]{2,1,0:T(2,128)(2,1)} %shard_map.262) | data formatting | bytes 131072

commit v2 on v1

--- a/solution.py
+++ b/solution.py
@@ -146,6 +146,45 @@
     lon = lax.axis_index("lon")
     lat_rows, lon_cols = grid_hbm.shape[:2]
 
+    def place(step_lat, step_lon, sign):
+        return (
+            (lat + sign * step_lat + LATS) & (LATS - 1),
+            (lon + sign * step_lon + LONS) & (LONS - 1),
+        )
+
+    def for_all_others(act):
+        for step_lon in range(1, LONS):
+            act(0, step_lon)
+
+        def band(step_lat, carry):
+            for step_lon in range(LONS):
+                act(step_lat, step_lon)
+            return carry
+
+        lax.fori_loop(1, LATS, band, 0)
+
+    barrier = pltpu.get_barrier_semaphore()
+    for i in NEAR:
+        pl.semaphore_signal(
+            barrier, inc=1, device_id=place(i // LONS, i % LONS, 1), device_id_type=MESH
+        )
+
+    def greet(step_lat, step_lon):
+        pl.semaphore_signal(
+            barrier, inc=1, device_id=place(step_lat, step_lon, 1), device_id_type=MESH
+        )
+
+    for step_lat in (0, 1, LATS - 1):
+        for step_lon in range(2, LONS - 1):
+            greet(step_lat, step_lon)
+
+    def greet_band(step_lat, carry):
+        for step_lon in range(LONS):
+            greet(step_lat, step_lon)
+        return carry
+
+    lax.fori_loop(2, LATS - 1, greet_band, 0)
+
     sender_copy = pltpu.make_async_copy(sender_hbm, sender, sender_sem)
     sender_copy.start()
     fetches = [
@@ -165,32 +204,6 @@
     cells_copy.start()
     for copy in fetches[3:]:
         copy.start()
-
-    def place(step_lat, step_lon, sign):
-        return (
-            (lat + sign * step_lat + LATS) & (LATS - 1),
-            (lon + sign * step_lon + LONS) & (LONS - 1),
-        )
-
-    def for_all_others(act):
-        for step_lon in range(1, LONS):
-            act(0, step_lon)
-
-        def band(step_lat, carry):
-            for step_lon in range(LONS):
-                act(step_lat, step_lon)
-            return carry
-
-        lax.fori_loop(1, LATS, band, 0)
-
-    barrier = pltpu.get_barrier_semaphore()
-
-    def greet(step_lat, step_lon):
-        pl.semaphore_signal(
-            barrier, inc=1, device_id=place(step_lat, step_lon, 1), device_id_type=MESH
-        )
-
-    for_all_others(greet)
 
     ready(fetch.g2m_receiver, fetch.mesh_sender, fetch.mesh_receiver)
     senders = held.mesh_sender[...]
@@ -256,30 +269,6 @@
 
     for_all_others(ask)
 
-    owner1 = hot(iota((PAIRS, EDGES), 0) == rel)
-    row1 = iota((NODES, EDGES), 0) == row
-    needed = hot(mm_nt(hot(row1), owner1) > 0.5)
-    below = hot(iota((NODES, NODES), 1) < iota((NODES, NODES), 0))
-    order = mm(below, needed).astype(BF)
-    rank = jnp.sum(jnp.where(row1, mm(order, owner1), 0.0), axis=0, keepdims=True).astype(I32)
-    near = jnp.zeros_like(rel)
-    for n, i in enumerate(NEAR):
-        near = jnp.where(rel == i, n, near)
-    slot = jnp.where(rank == 0, rel, PAIRS + EXTRA * near + rank - 1)
-    slot = jnp.where(rel == 0, SLOTS + row, slot)
-    slot_column = doubled_column(slot, EDGES)
-    shape = (2 * EDGES, 2 * (SLOTS + NODES))
-    gather = hot(iota(shape, 1) == 2 * slot_column + (iota(shape, 0) & 1))
-    gather_far[...] = gather[:, : 2 * SLOTS]
-    gather_own[...] = gather[:, 2 * SLOTS :]
-    receivers = held.mesh_receiver[...]
-    shape = (2 * EDGES, 2 * NODES)
-    gather_recv[...] = hot(
-        iota(shape, 1) == 2 * doubled_column(receivers, EDGES) + (iota(shape, 0) & 1)
-    )
-    shape = (2 * NODES, 2 * EDGES)
-    total_mesh = hot(iota(shape, 0) == 2 * doubled_row(receivers, EDGES) + (iota(shape, 1) & 1))
-
     grid_receivers = held.g2m_receiver[...]
     shape = (2 * NODES, 2 * GRID_EDGES)
     total_grid = hot(
@@ -300,11 +289,6 @@
     )
     shape = (2 * NODES, NODES)
     state = mm(hot(iota(shape, 1) == (iota(shape, 0) >> 1)), latents).astype(BF)
-    ready(fetch.mesh_edges)
-    shape = (2 * EDGES, EDGES)
-    edge_state = mm(
-        hot(iota(shape, 1) == (iota(shape, 0) >> 1)), held.mesh_edges[...]
-    ).astype(BF)
 
     sender_copy.wait()
     cells_copy.wait()
@@ -340,20 +324,6 @@
     latent = norm(mm(hidden, held.embed_w2[...]), held.embed_gain[...]).astype(BF)
     preact = mm(latent, held.enc_edge_w1[1]) + grid_base
     hidden = silu(preact).astype(BF)
-    ready(fetch.enc_edge_w2, fetch.enc_edge_gain)
-    update = norm(mm(hidden, held.enc_edge_w2[...]), held.enc_edge_gain[...])
-    new_edges = (grid_edges.astype(F32) + update).astype(BF)
-    summed = mm(total_grid, new_edges).astype(BF)
-    ready(fetch.enc_node_w1, fetch.enc_node_b1, fetch.enc_node_w2, fetch.enc_node_gain)
-    preact = (
-        mm(state, held.enc_node_w1[0])
-        + mm(summed, held.enc_node_w1[1])
-        + held.enc_node_b1[...]
-    )
-    hidden = silu(preact).astype(BF)
-    update = norm(mm(hidden, held.enc_node_w2[...]), held.enc_node_gain[...])
-    state = (state.astype(F32) + update).astype(BF)
-
     pltpu.make_async_copy(
         req_in.at[pl.ds(1, PAIRS - 1)], req_in.at[pl.ds(1, PAIRS - 1)], req_recv
     ).wait()
@@ -378,6 +348,20 @@
     pick_all[: 2 * PAIRS] = first
     pick_all[2 * PAIRS :] = more
 
+    ready(fetch.enc_edge_w2, fetch.enc_edge_gain)
+    update = norm(mm(hidden, held.enc_edge_w2[...]), held.enc_edge_gain[...])
+    new_edges = (grid_edges.astype(F32) + update).astype(BF)
+    summed = mm(total_grid, new_edges).astype(BF)
+    ready(fetch.enc_node_w1, fetch.enc_node_b1, fetch.enc_node_w2, fetch.enc_node_gain)
+    preact = (
+        mm(state, held.enc_node_w1[0])
+        + mm(summed, held.enc_node_w1[1])
+        + held.enc_node_b1[...]
+    )
+    hidden = silu(preact).astype(BF)
+    update = norm(mm(hidden, held.enc_node_w2[...]), held.enc_node_gain[...])
+    state = (state.astype(F32) + update).astype(BF)
+
     ready(fetch.proc_edge_w1, fetch.proc_edge_b1, fetch.proc_edge_w2, fetch.proc_edge_gain)
     ready(fetch.proc_node_w1, fetch.proc_node_b1, fetch.proc_node_w2, fetch.proc_node_gain)
     for t in range(STEPS):
@@ -400,6 +384,37 @@
                 send_sem=row_send.at[t], recv_sem=row_recv.at[t],
                 device_id=place(i // LONS, i % LONS, -1), device_id_type=MESH,
             ).start()
+
+        if t == 0:
+            owner1 = hot(iota((PAIRS, EDGES), 0) == rel)
+            row1 = iota((NODES, EDGES), 0) == row
+            needed = hot(mm_nt(hot(row1), owner1) > 0.5)
+            below = hot(iota((NODES, NODES), 1) < iota((NODES, NODES), 0))
+            order = mm(below, needed).astype(BF)
+            rank = jnp.sum(jnp.where(row1, mm(order, owner1), 0.0), axis=0, keepdims=True).astype(I32)
+            near = jnp.zeros_like(rel)
+            for n, i in enumerate(NEAR):
+                near = jnp.where(rel == i, n, near)
+            slot = jnp.where(rank == 0, rel, PAIRS + EXTRA * near + rank - 1)
+            slot = jnp.where(rel == 0, SLOTS + row, slot)
+            slot_column = doubled_column(slot, EDGES)
+            shape = (2 * EDGES, 2 * (SLOTS + NODES))
+            gather = hot(iota(shape, 1) == 2 * slot_column + (iota(shape, 0) & 1))
+            gather_far[...] = gather[:, : 2 * SLOTS]
+            gather_own[...] = gather[:, 2 * SLOTS :]
+            receivers = held.mesh_receiver[...]
+            shape = (2 * EDGES, 2 * NODES)
+            gather_recv[...] = hot(
+                iota(shape, 1) == 2 * doubled_column(receivers, EDGES) + (iota(shape, 0) & 1)
+            )
+            shape = (2 * NODES, 2 * EDGES)
+            total_mesh = hot(iota(shape, 0) == 2 * doubled_row(receivers, EDGES) + (iota(shape, 1) & 1))
+
+            ready(fetch.mesh_edges)
+            shape = (2 * EDGES, EDGES)
+            edge_state = mm(
+                hot(iota(shape, 1) == (iota(shape, 0) >> 1)), held.mesh_edges[...]
+            ).astype(BF)
 
         incoming = mm(state, held.proc_edge_w1[t, 2]).astype(BF)
         edge_base[...] = (
@@ -421,7 +436,7 @@
         update = norm(mm(hidden, held.proc_node_w2[t]), held.proc_node_gain[t : t + 1])
         state = (state.astype(F32) + update).astype(BF)
 
-    out_ref[...] = state.reshape(NODES, 2, D)
+    out_ref[...] = state
 
     for copy in groups[0]:
         copy.wait_send()
@@ -506,7 +521,7 @@
     ]
     return pl.pallas_call(
         kernel,
-        out_shape=jax.ShapeDtypeStruct((NODES, batch, D), BF),
+        out_shape=jax.ShapeDtypeStruct((NODES * batch, D), BF),
         in_specs=[pl.BlockSpec(memory_space=pl.ANY)] * len(operands),
         out_specs=pl.BlockSpec(memory_space=pltpu.VMEM),
         scratch_shapes=scratch,
@@ -516,7 +531,7 @@
         compiler_params=pltpu.CompilerParams(
             collective_id=0, has_side_effects=True, vmem_limit_bytes=64 * 2**20
         ),
-    )(*operands)
+    )(*operands).reshape(NODES, batch, D)
 
 
 def solution(mesh):

time: 42.5 us -> 42.4 us (level)
    unnamed x1 -> x0, local copies, waits for them, and re-layouts: 1.52 us -> none
    reshape x0 -> x1, local copies, waits for them, and re-layouts: none -> 1.5 us  [on_device(): return pl.pallas_call(kernel, out_shape=jax.ShapeDtypeStruct((NODES * bat...]
where the time goes in v2:
time: 42.4 us; the launch traced here: 42.3 us
  Pallas kernels  40.7 us (96%)
  local copies, waits for them, and re-layouts  1.5 us (4%)
    pallas_call x1, Pallas kernels, on_device(): pl.pallas_call(kernel, out_shape=jax.ShapeDtypeStruct((NODES * batch, D),...  40.7 us
    reshape x1, local copies, waits for them, and re-layouts, on_device(): return pl.pallas_call(kernel, out_shape=jax.ShapeDtypeStruct((NODES * bat...  1.5 us

profile of v2, /device:TPU:1, one launch (start us, length us, event | category | flops | bytes accessed | tf_op | source)
XLA Modules:
  0.0 42.3 jit_solution(10777943438700056086)
XLA Ops:
  0.0 40.7 %shard_map.262 = bf16[64,512]{1,0:T(8,128)(2,1)} custom-call(bf16[48,64,2,227]{3,2,1,0:T(2,128)(2,1)} %refs_0_.1, s32[128]{0:T(128)} %refs_1_.1, s32[1,128]{1,0:T(1,128)} %bitcast.17, s32[1,256]{1,0:T(1,128)} %bitcast.15, s32[1,256]{1,0:T(1,128)} %bitcast.16, bf16[32,512]{1,0:T(8,128)(2,1)} %refs_5_.1, bf16[128,512]{1,0:T(8,128)(2,1)} %refs_6_.1, ...), custom_call_target="tpu_custom_call" | custom-call | flops 4000000000 | bytes 15000000 | tf_op jit(solution)/shard_map/pallas_call | solution.py:522
  40.8 1.5 %reshape.39 = bf16[32,2,512]{2,1,0:T(2,128)(2,1)} reshape(bf16[64,512]{1,0:T(8,128)(2,1)} %shard_map.262) | data formatting | bytes 131072 | tf_op jit(solution)/shard_map/reshape | solution.py:534

commit v3 on v2

--- a/solution.py
+++ b/solution.py
@@ -18,13 +18,18 @@
 STEPS = 2
 LATS = 8
 LONS = 16
-PAIRS = LATS * LONS
+CORES = 2
+XS = LATS // CORES
+CHIPS = XS * LONS
 NODES = 32
+CHIP_NODES = CORES * NODES
 GRID_EDGES = 128
 EDGES = 256
-NEAR = (1, 15, 16, 17, 31, 112, 113, 127)
-EXTRA = 3
-SLOTS = PAIRS + EXTRA * len(NEAR)
+PLAIN = 2 * CHIPS
+NEAR = (1, 15, 16, 17, 31, 48, 49, 63)
+EXTRA = (6, 6, 3, 3, 3, 3, 3, 3)
+START = (0, 6, 12, 15, 18, 21, 24, 27)
+SLOTS = PLAIN + sum(EXTRA)
 DIRECTIONS = tuple((a, b) for a in (0, -1, 1) for b in (0, -1, 1) if (a, b) != (0, 0))
 
 
@@ -137,53 +142,50 @@
     held = Held(*refs[:FETCHED])
     (
         cells, sender, picked, pick_all, gather_far, gather_own, gather_recv, edge_base,
-        req_out, req_in, out_rows, in_rows,
+        req_out, req_in, chip_rows, out_rows, in_rows,
         fetch_sem, cells_sem, sender_sem,
-        halo_send, halo_recv, req_send, req_recv, row_send, row_recv,
+        halo_send, halo_recv, req_send, req_recv, share_send, share_recv,
+        row_send, row_recv,
     ) = refs[FETCHED:]
 
     lat = lax.axis_index("lat")
     lon = lax.axis_index("lon")
     lat_rows, lon_cols = grid_hbm.shape[:2]
 
-    def place(step_lat, step_lon, sign):
+    core = lat & 1
+    beside = lat ^ 1
+
+    def place(step_x, step_lon, sign):
         return (
-            (lat + sign * step_lat + LATS) & (LATS - 1),
+            (lat + sign * CORES * step_x + LATS) & (LATS - 1),
             (lon + sign * step_lon + LONS) & (LONS - 1),
         )
 
-    def for_all_others(act):
+    def for_all_chips(act):
         for step_lon in range(1, LONS):
             act(0, step_lon)
 
-        def band(step_lat, carry):
+        def band(step_x, carry):
             for step_lon in range(LONS):
-                act(step_lat, step_lon)
+                act(step_x, step_lon)
             return carry
 
-        lax.fori_loop(1, LATS, band, 0)
+        lax.fori_loop(1, XS, band, 0)
 
     barrier = pltpu.get_barrier_semaphore()
-    for i in NEAR:
+    others = [(a, b) for a in (-1, 1) for b in (0, -1, 1)]
+    for a, b in others:
         pl.semaphore_signal(
-            barrier, inc=1, device_id=place(i // LONS, i % LONS, 1), device_id_type=MESH
+            barrier, inc=1, device_id_type=MESH,
+            device_id=((lat + a + LATS) & (LATS - 1), (lon + b + LONS) & (LONS - 1)),
         )
 
-    def greet(step_lat, step_lon):
+    def greet(step_x, step_lon):
         pl.semaphore_signal(
-            barrier, inc=1, device_id=place(step_lat, step_lon, 1), device_id_type=MESH
+            barrier, inc=1, device_id=place(step_x, step_lon, 1), device_id_type=MESH
         )
 
-    for step_lat in (0, 1, LATS - 1):
-        for step_lon in range(2, LONS - 1):
-            greet(step_lat, step_lon)
-
-    def greet_band(step_lat, carry):
-        for step_lon in range(LONS):
-            greet(step_lat, step_lon)
-        return carry
-
-    lax.fori_loop(2, LATS - 1, greet_band, 0)
+    for_all_chips(greet)
 
     sender_copy = pltpu.make_async_copy(sender_hbm, sender, sender_sem)
     sender_copy.start()
@@ -198,30 +200,25 @@
 
     for copy in fetches[:3]:
         copy.start()
-    cells_copy = pltpu.make_async_copy(
-        grid_hbm, cells.at[pl.ds(HALO, lat_rows), pl.ds(HALO, lon_cols)], cells_sem
-    )
-    cells_copy.start()
-    for copy in fetches[3:]:
-        copy.start()
-
     ready(fetch.g2m_receiver, fetch.mesh_sender, fetch.mesh_receiver)
     senders = held.mesh_sender[...]
     owner = senders >> 5
-    row = senders & (NODES - 1)
-    rel = ((((owner >> 4) - lat) & (LATS - 1)) << 4) | (((owner & 15) - lon) & (LONS - 1))
-    owner2 = hot((iota((2 * PAIRS, EDGES), 0) >> 1) == rel)
-    row2 = hot((iota((128, EDGES), 0) >> 1) == row)
-    asked = mm_nt(owner2, row2)
-    shape = (2 * PAIRS, 128)
+    step_x = ((owner >> 5) - (lat >> 1)) & (XS - 1)
+    rel = (step_x << 4) | (((owner & 15) - lon) & (LONS - 1))
+    row = (((owner >> 4) & 1) << 5) | (senders & (NODES - 1))
+    shape = (2 * CHIPS, EDGES)
+    chip2 = hot((iota(shape, 0) >> 1) == rel)
+    row2 = hot((iota(shape, 0) >> 1) == row)
+    shape = (2 * CHIPS, 2 * CHIP_NODES)
     same = (iota(shape, 0) & 1) == (iota(shape, 1) & 1)
-    asked = hot((asked > 0.5) & same & (iota(shape, 0) >= 2))
-    req_out[...] = asked.reshape(PAIRS, 2, 128)
-    req_in[0] = jnp.zeros((2, 128), BF)
+    asked = hot((mm_nt(chip2, row2) > 0.5) & same & (iota(shape, 0) >= 2))
+    req_out[...] = asked.reshape(CHIPS, 2, 2 * CHIP_NODES)
+    req_in[0] = jnp.zeros((2, 2 * CHIP_NODES), BF)
     for t in range(STEPS):
         in_rows[t, 0] = jnp.zeros((2, D), BF)
-
-    pl.semaphore_wait(barrier, PAIRS - 1)
+        in_rows[t, 1] = jnp.zeros((2, D), BF)
+
+    pl.semaphore_wait(barrier, CHIPS - 1 + len(others))
 
     spans = {0: (0, lat_rows, HALO), -1: (0, HALO, HALO + lat_rows), 1: (lat_rows - HALO, HALO, 0)}
     spans_lon = {
@@ -260,14 +257,21 @@
         for copy in groups[2]:
             copy.start()
 
-    def ask(step_lat, step_lon):
-        i = step_lat * LONS + step_lon
+    cells_copy = pltpu.make_async_copy(
+        grid_hbm, cells.at[pl.ds(HALO, lat_rows), pl.ds(HALO, lon_cols)], cells_sem
+    )
+    cells_copy.start()
+    for copy in fetches[3:]:
+        copy.start()
+
+    def ask(step_x, step_lon):
+        i = step_x * LONS + step_lon
         pltpu.make_async_remote_copy(
             src_ref=req_out.at[i], dst_ref=req_in.at[i], send_sem=req_send, recv_sem=req_recv,
-            device_id=place(step_lat, step_lon, 1), device_id_type=MESH,
+            device_id=place(step_x, step_lon, 1), device_id_type=MESH,
         ).start()
 
-    for_all_others(ask)
+    for_all_chips(ask)
 
     grid_receivers = held.g2m_receiver[...]
     shape = (2 * NODES, 2 * GRID_EDGES)
@@ -324,29 +328,26 @@
     latent = norm(mm(hidden, held.embed_w2[...]), held.embed_gain[...]).astype(BF)
     preact = mm(latent, held.enc_edge_w1[1]) + grid_base
     hidden = silu(preact).astype(BF)
-    pltpu.make_async_copy(
-        req_in.at[pl.ds(1, PAIRS - 1)], req_in.at[pl.ds(1, PAIRS - 1)], req_recv
-    ).wait()
-    wanted = req_in[...].reshape(2 * PAIRS, 128)[:, : 2 * NODES]
-    shape = (2 * NODES, 2 * NODES)
+    asked_all = req_in.at[pl.ds(1, CHIPS - 1)]
+    pltpu.make_async_copy(asked_all, asked_all, req_recv).wait()
+    wanted = req_in[...].reshape(2 * CHIPS, 2 * CHIP_NODES)
+    shape = (2 * CHIP_NODES, 2 * CHIP_NODES)
     before = hot(
         (iota(shape, 0) < iota(shape, 1)) & ((iota(shape, 0) & 1) == (iota(shape, 1) & 1))
     )
     place_of = mm(wanted, before).astype(BF)
-    first = jnp.where(place_of.astype(F32) < 0.5, wanted.astype(F32), 0.0).astype(BF)
-    shape = (2 * EXTRA * len(NEAR), 2 * PAIRS)
+    shape = (2 * SLOTS, 2 * CHIPS)
     line = iota(shape, 0)
-    which = jnp.zeros_like(line)
-    target = jnp.full_like(line, NEAR[0])
-    for n in range(1, len(NEAR)):
-        later = line >= 2 * EXTRA * n
-        which = jnp.where(later, n, which)
-        target = jnp.where(later, NEAR[n], target)
-    choose = hot(iota(shape, 1) == 2 * target + (line & 1))
-    kth = ((line >> 1) - EXTRA * which + 1).astype(F32)[:, : 2 * NODES]
-    more = jnp.where(mm(choose, place_of) == kth, mm(choose, wanted), 0.0).astype(BF)
-    pick_all[: 2 * PAIRS] = first
-    pick_all[2 * PAIRS :] = more
+    number = line >> 1
+    chip = number >> 1
+    kth = number & 1
+    for i, start in zip(NEAR, START):
+        later = number >= PLAIN + start
+        chip = jnp.where(later, i, chip)
+        kth = jnp.where(later, number - (PLAIN + start - 2), kth)
+    choose = hot(iota(shape, 1) == 2 * chip + (line & 1))
+    kth = kth.astype(F32)
+    pick_all[...] = jnp.where(mm(choose, place_of) == kth, mm(choose, wanted), 0.0).astype(BF)
 
     ready(fetch.enc_edge_w2, fetch.enc_edge_gain)
     update = norm(mm(hidden, held.enc_edge_w2[...]), held.enc_edge_gain[...])
@@ -365,40 +366,52 @@
     ready(fetch.proc_edge_w1, fetch.proc_edge_b1, fetch.proc_edge_w2, fetch.proc_edge_gain)
     ready(fetch.proc_node_w1, fetch.proc_node_b1, fetch.proc_node_w2, fetch.proc_node_gain)
     for t in range(STEPS):
-        outgoing = mm(state, held.proc_edge_w1[t, 1]).astype(BF)
+        chip_rows[t, core] = mm(state, held.proc_edge_w1[t, 1]).astype(BF)
+        share = pltpu.make_async_remote_copy(
+            src_ref=chip_rows.at[t, core], dst_ref=chip_rows.at[t, core],
+            send_sem=share_send.at[t], recv_sem=share_recv.at[t],
+            device_id=(beside, lon), device_id_type=MESH,
+        )
+        share.start()
+        incoming = mm(state, held.proc_edge_w1[t, 2]).astype(BF)
+        node_base = mm(state, held.proc_node_w1[t, 0]) + held.proc_node_b1[t : t + 1]
+        share.wait()
+        outgoing = chip_rows[t].reshape(2 * CHIP_NODES, D)
         out_rows[t] = mm(pick_all[...], outgoing).astype(BF).reshape(SLOTS, 2, D)
 
-        def give(step_lat, step_lon, t=t):
-            i = step_lat * LONS + step_lon
-            pltpu.make_async_remote_copy(
-                src_ref=out_rows.at[t, i], dst_ref=in_rows.at[t, i],
-                send_sem=row_send.at[t], recv_sem=row_recv.at[t],
-                device_id=place(step_lat, step_lon, -1), device_id_type=MESH,
-            ).start()
-
-        for_all_others(give)
         for n, i in enumerate(NEAR):
-            span = pl.ds(PAIRS + EXTRA * n, EXTRA)
+            span = pl.ds(PLAIN + START[n], EXTRA[n])
             pltpu.make_async_remote_copy(
                 src_ref=out_rows.at[t, span], dst_ref=in_rows.at[t, span],
                 send_sem=row_send.at[t], recv_sem=row_recv.at[t],
                 device_id=place(i // LONS, i % LONS, -1), device_id_type=MESH,
             ).start()
 
+        def give(step_x, step_lon, t=t):
+            span = pl.ds(2 * (step_x * LONS + step_lon), 2)
+            pltpu.make_async_remote_copy(
+                src_ref=out_rows.at[t, span], dst_ref=in_rows.at[t, span],
+                send_sem=row_send.at[t], recv_sem=row_recv.at[t],
+                device_id=place(step_x, step_lon, -1), device_id_type=MESH,
+            ).start()
+
+        for_all_chips(give)
+
         if t == 0:
-            owner1 = hot(iota((PAIRS, EDGES), 0) == rel)
-            row1 = iota((NODES, EDGES), 0) == row
-            needed = hot(mm_nt(hot(row1), owner1) > 0.5)
-            below = hot(iota((NODES, NODES), 1) < iota((NODES, NODES), 0))
-            order = mm(below, needed).astype(BF)
-            rank = jnp.sum(jnp.where(row1, mm(order, owner1), 0.0), axis=0, keepdims=True).astype(I32)
-            near = jnp.zeros_like(rel)
-            for n, i in enumerate(NEAR):
-                near = jnp.where(rel == i, n, near)
-            slot = jnp.where(rank == 0, rel, PAIRS + EXTRA * near + rank - 1)
+            chip1 = hot(iota((CHIPS, EDGES), 0) == rel)
+            row1 = iota((CHIP_NODES, EDGES), 0) == row
+            needed = hot(mm_nt(hot(row1), chip1) > 0.5)
+            shape = (CHIP_NODES, CHIP_NODES)
+            order = mm(hot(iota(shape, 1) < iota(shape, 0)), needed).astype(BF)
+            rank = jnp.where(row1, mm(order, chip1), 0.0)
+            rank = jnp.sum(rank, axis=0, keepdims=True).astype(I32)
+            extra = jnp.zeros_like(rel)
+            for i, start in zip(NEAR, START):
+                extra = jnp.where(rel == i, start, extra)
+            slot = jnp.where(rank < 2, 2 * rel + rank, PLAIN + extra + rank - 2)
             slot = jnp.where(rel == 0, SLOTS + row, slot)
             slot_column = doubled_column(slot, EDGES)
-            shape = (2 * EDGES, 2 * (SLOTS + NODES))
+            shape = (2 * EDGES, 2 * (SLOTS + CHIP_NODES))
             gather = hot(iota(shape, 1) == 2 * slot_column + (iota(shape, 0) & 1))
             gather_far[...] = gather[:, : 2 * SLOTS]
             gather_own[...] = gather[:, 2 * SLOTS :]
@@ -416,16 +429,13 @@
                 hot(iota(shape, 1) == (iota(shape, 0) >> 1)), held.mesh_edges[...]
             ).astype(BF)
 
-        incoming = mm(state, held.proc_edge_w1[t, 2]).astype(BF)
         edge_base[...] = (
             mm(edge_state, held.proc_edge_w1[t, 0])
             + mm(gather_recv[...], incoming)
             + mm(gather_own[...], outgoing)
             + held.proc_edge_b1[t : t + 1]
         )
-        node_base = mm(state, held.proc_node_w1[t, 0]) + held.proc_node_b1[t : t + 1]
-
-        arrived = in_rows.at[t, pl.ds(1, SLOTS - 1)]
+        arrived = in_rows.at[t, pl.ds(2, SLOTS - 2)]
         pltpu.make_async_copy(arrived, arrived, row_recv.at[t]).wait()
         table = in_rows[t].reshape(2 * SLOTS, D)
         hidden = silu(edge_base[...] + mm(gather_far[...], table)).astype(BF)
@@ -451,10 +461,10 @@
         for copy in groups[2]:
             copy.wait_send()
 
-    asked_all = req_out.at[pl.ds(1, PAIRS - 1)]
+    asked_all = req_out.at[pl.ds(1, CHIPS - 1)]
     pltpu.make_async_copy(asked_all, asked_all, req_send).wait()
     for t in range(STEPS):
-        sent = out_rows.at[t, pl.ds(1, SLOTS - 1)]
+        sent = out_rows.at[t, pl.ds(2, SLOTS - 2)]
         pltpu.make_async_copy(sent, sent, row_send.at[t]).wait()
 
 
@@ -500,13 +510,14 @@
         pltpu.VMEM((lat_rows + 2 * HALO, lon_cols + 2 * HALO, batch, width), BF),
         pltpu.SMEM((GRID_EDGES,), I32),
         pltpu.VMEM((GRID_EDGES, batch, width), BF),
-        pltpu.VMEM((2 * SLOTS, 2 * NODES), BF),
+        pltpu.VMEM((2 * SLOTS, 2 * CHIP_NODES), BF),
         pltpu.VMEM((2 * EDGES, 2 * SLOTS), BF),
-        pltpu.VMEM((2 * EDGES, 2 * NODES), BF),
+        pltpu.VMEM((2 * EDGES, 2 * CHIP_NODES), BF),
         pltpu.VMEM((2 * EDGES, 2 * NODES), BF),
         pltpu.VMEM((2 * EDGES, D), F32),
-        pltpu.VMEM((PAIRS, 2, 128), BF),
-        pltpu.VMEM((PAIRS, 2, 128), BF),
+        pltpu.VMEM((CHIPS, 2, 2 * CHIP_NODES), BF),
+        pltpu.VMEM((CHIPS, 2, 2 * CHIP_NODES), BF),
+        pltpu.VMEM((STEPS, CORES, 2 * NODES, D), BF),
         pltpu.VMEM((STEPS, SLOTS, 2, D), BF),
         pltpu.VMEM((STEPS, SLOTS, 2, D), BF),
         dma((FETCHED,)),
@@ -516,6 +527,8 @@
         dma((len(DIRECTIONS),)),
         dma,
         dma,
+        dma((STEPS,)),
+        dma((STEPS,)),
         dma((STEPS,)),
         dma((STEPS,)),
     ]

time: 42.4 us -> 44.5 us (1.050)
  Pallas kernels: 40.7 us -> 42.8 us
    pallas_call x1, Pallas kernels: 40.7 us -> 42.8 us  [on_device(): pl.pallas_call(kernel, out_shape=jax.ShapeDtypeStruct((NODES * batch, D),...]
where the time goes in v3:
time: 44.5 us; the launch traced here: 44.3 us
  Pallas kernels  42.8 us (96%)
  local copies, waits for them, and re-layouts  1.5 us (3%)
    pallas_call x1, Pallas kernels, on_device(): pl.pallas_call(kernel, out_shape=jax.ShapeDtypeStruct((NODES * batch, D),...  42.8 us
    reshape x1, local copies, waits for them, and re-layouts, on_device(): return pl.pallas_call(kernel, out_shape=jax.ShapeDtypeStruct((NODES * bat...  1.5 us

profile of v3, /device:TPU:1, one launch (start us, length us, event | category | flops | bytes accessed | tf_op | source)
XLA Modules:
  0.0 44.3 jit_solution(14054748289191453243)
XLA Ops:
  0.0 42.8 %shard_map.262 = bf16[64,512]{1,0:T(8,128)(2,1)} custom-call(bf16[48,64,2,227]{3,2,1,0:T(2,128)(2,1)} %refs_0_.1, s32[128]{0:T(128)} %refs_1_.1, s32[1,128]{1,0:T(1,128)} %bitcast.17, s32[1,256]{1,0:T(1,128)} %bitcast.15, s32[1,256]{1,0:T(1,128)} %bitcast.16, bf16[32,512]{1,0:T(8,128)(2,1)} %refs_5_.1, bf16[128,512]{1,0:T(8,128)(2,1)} %refs_6_.1, ...), custom_call_target="tpu_custom_call" | custom-call | flops 4000000000 | bytes 15000000 | tf_op jit(solution)/shard_map/pallas_call | solution.py:535
  42.8 1.5 %reshape.39 = bf16[32,2,512]{2,1,0:T(2,128)(2,1)} reshape(bf16[64,512]{1,0:T(8,128)(2,1)} %shard_map.262) | data formatting | bytes 131072 | tf_op jit(solution)/shard_map/reshape | solution.py:547

commit v4 on v2

--- a/solution.py
+++ b/solution.py
@@ -16,6 +16,7 @@
 D = 512
 HALO = 2
 STEPS = 2
+CHUNK = 64
 LATS = 8
 LONS = 16
 PAIRS = LATS * LONS
@@ -118,6 +119,20 @@
     return centered * lax.rsqrt(variance + 1e-05) * gain
 
 
+def by_rows(act, *arrays):
+    count = arrays[0].shape[0]
+    pieces = [act(*(v[c : c + CHUNK] for v in arrays)) for c in range(0, count, CHUNK)]
+    return jnp.concatenate(pieces, axis=0)
+
+
+def silu_rows(*terms):
+    return by_rows(lambda *parts: silu(sum(parts[1:], parts[0])).astype(BF), *terms)
+
+
+def updated_rows(rows, v, gain):
+    return by_rows(lambda r, part: (r.astype(F32) + norm(part, gain)).astype(BF), rows, v)
+
+
 def doubled_column(row, count):
     shape = (2 * count, count)
     spread = jnp.where(iota(shape, 1) == (iota(shape, 0) >> 1), row.astype(F32), 0.0)
@@ -309,21 +324,22 @@
 
     def pick(k, carry):
         cell = sender[k]
-        cell_row = (cell // width) - lat * lat_rows + HALO
+        cell_row = (cell >> 10) - lat * lat_rows + HALO
         cell_col = ((cell & (width - 1)) - lon * lon_cols + HALO + width) & (width - 1)
         cell_row = jnp.clip(cell_row, 0, cells.shape[0] - 1)
         cell_col = jnp.clip(cell_col, 0, cells.shape[1] - 1)
         picked[k] = cells[cell_row, cell_col]
         return carry
 
-    lax.fori_loop(0, GRID_EDGES, pick, 0, unroll=8)
+    lax.fori_loop(0, GRID_EDGES, pick, 0, unroll=16)
 
     ready(fetch.embed_w1, fetch.embed_b1, fetch.embed_w2, fetch.embed_gain)
     inputs = picked[...].reshape(2 * GRID_EDGES, picked.shape[2])
-    hidden = silu(mm(inputs, held.embed_w1[...]) + held.embed_b1[...]).astype(BF)
-    latent = norm(mm(hidden, held.embed_w2[...]), held.embed_gain[...]).astype(BF)
-    preact = mm(latent, held.enc_edge_w1[1]) + grid_base
-    hidden = silu(preact).astype(BF)
+    bias = held.embed_b1[...]
+    hidden = by_rows(lambda v: silu(v + bias).astype(BF), mm(inputs, held.embed_w1[...]))
+    gain = held.embed_gain[...]
+    latent = by_rows(lambda v: norm(v, gain).astype(BF), mm(hidden, held.embed_w2[...]))
+    hidden = silu_rows(mm(latent, held.enc_edge_w1[1]), grid_base)
     pltpu.make_async_copy(
         req_in.at[pl.ds(1, PAIRS - 1)], req_in.at[pl.ds(1, PAIRS - 1)], req_recv
     ).wait()
@@ -349,8 +365,7 @@
     pick_all[2 * PAIRS :] = more
 
     ready(fetch.enc_edge_w2, fetch.enc_edge_gain)
-    update = norm(mm(hidden, held.enc_edge_w2[...]), held.enc_edge_gain[...])
-    new_edges = (grid_edges.astype(F32) + update).astype(BF)
+    new_edges = updated_rows(grid_edges, mm(hidden, held.enc_edge_w2[...]), held.enc_edge_gain[...])
     summed = mm(total_grid, new_edges).astype(BF)
     ready(fetch.enc_node_w1, fetch.enc_node_b1, fetch.enc_node_w2, fetch.enc_node_gain)
     preact = (
@@ -428,9 +443,12 @@
         arrived = in_rows.at[t, pl.ds(1, SLOTS - 1)]
         pltpu.make_async_copy(arrived, arrived, row_recv.at[t]).wait()
         table = in_rows[t].reshape(2 * SLOTS, D)
-        hidden = silu(edge_base[...] + mm(gather_far[...], table)).astype(BF)
-        update = norm(mm(hidden, held.proc_edge_w2[t]), held.proc_edge_gain[t : t + 1])
-        edge_state = (edge_state.astype(F32) + update).astype(BF)
+        gain = held.proc_edge_gain[t : t + 1]
+        halves = []
+        for span in (slice(0, EDGES), slice(EDGES, 2 * EDGES)):
+            hidden = silu_rows(mm(gather_far[span], table), edge_base[span])
+            halves.append(updated_rows(edge_state[span], mm(hidden, held.proc_edge_w2[t]), gain))
+        edge_state = jnp.concatenate(halves, axis=0)
         summed = mm(total_mesh, edge_state).astype(BF)
         hidden = silu(node_base + mm(summed, held.proc_node_w1[t, 1])).astype(BF)
         update = norm(mm(hidden, held.proc_node_w2[t]), held.proc_node_gain[t : t + 1])

time: 42.4 us -> 42.2 us (level)
  no operation moved by 1% of the time
where the time goes in v4:
time: 42.2 us; the launch traced here: 42 us
  Pallas kernels  40.5 us (96%)
  local copies, waits for them, and re-layouts  1.5 us (4%)
    pallas_call x1, Pallas kernels, on_device(): pl.pallas_call(kernel, out_shape=jax.ShapeDtypeStruct((NODES * batch, D),...  40.5 us
    reshape x1, local copies, waits for them, and re-layouts, on_device(): return pl.pallas_call(kernel, out_shape=jax.ShapeDtypeStruct((NODES * bat...  1.5 us

profile of v4, /device:TPU:1, one launch (start us, length us, event | category | flops | bytes accessed | tf_op | source)
XLA Modules:
  0.0 42.0 jit_solution(2546941567737040119)
XLA Ops:
  0.0 40.5 %shard_map.262 = bf16[64,512]{1,0:T(8,128)(2,1)} custom-call(bf16[48,64,2,227]{3,2,1,0:T(2,128)(2,1)} %refs_0_.1, s32[128]{0:T(128)} %refs_1_.1, s32[1,128]{1,0:T(1,128)} %bitcast.17, s32[1,256]{1,0:T(1,128)} %bitcast.15, s32[1,256]{1,0:T(1,128)} %bitcast.16, bf16[32,512]{1,0:T(8,128)(2,1)} %refs_5_.1, bf16[128,512]{1,0:T(8,128)(2,1)} %refs_6_.1, ...), custom_call_target="tpu_custom_call" | custom-call | flops 4000000000 | bytes 15000000 | tf_op jit(solution)/shard_map/pallas_call | solution.py:540
  40.5 1.5 %reshape.39 = bf16[32,2,512]{2,1,0:T(2,128)(2,1)} reshape(bf16[64,512]{1,0:T(8,128)(2,1)} %shard_map.262) | data formatting | bytes 131072 | tf_op jit(solution)/shard_map/reshape | solution.py:552

commit v5 on v4

--- a/solution.py
+++ b/solution.py
@@ -168,15 +168,19 @@
         )
 
     def for_all_others(act):
-        for step_lon in range(1, LONS):
-            act(0, step_lon)
-
-        def band(step_lat, carry):
-            for step_lon in range(LONS):
+        steps_lat = (0, 4, 1, 7, 2, 6, 3, 5)
+        for step_lat in steps_lat:
+            act(step_lat, 8)
+        for step_lat in steps_lat[1:]:
+            act(step_lat, 0)
+
+        def pair(step_lon, carry):
+            for step_lat in steps_lat:
                 act(step_lat, step_lon)
+                act(step_lat, LONS - step_lon)
             return carry
 
-        lax.fori_loop(1, LATS, band, 0)
+        lax.fori_loop(1, LONS // 2, pair, 0)
 
     barrier = pltpu.get_barrier_semaphore()
     for i in NEAR:

time: 42.2 us -> 42.9 us (1.017)
  Pallas kernels: 40.5 us -> 41.2 us
    pallas_call x1, Pallas kernels: 40.5 us -> 41.2 us  [on_device(): pl.pallas_call(kernel, out_shape=jax.ShapeDtypeStruct((NODES * batch, D),...]
where the time goes in v5:
time: 42.9 us; the launch traced here: 42.7 us
  Pallas kernels  41.2 us (96%)
  local copies, waits for them, and re-layouts  1.5 us (3%)
    pallas_call x1, Pallas kernels, on_device(): pl.pallas_call(kernel, out_shape=jax.ShapeDtypeStruct((NODES * batch, D),...  41.2 us
    reshape x1, local copies, waits for them, and re-layouts, on_device(): return pl.pallas_call(kernel, out_shape=jax.ShapeDtypeStruct((NODES * bat...  1.5 us

profile of v5, /device:TPU:1, one launch (start us, length us, event | category | flops | bytes accessed | tf_op | source)
XLA Modules:
  0.0 42.7 jit_solution(5301329563960597903)
XLA Ops:
  0.0 41.2 %shard_map.262 = bf16[64,512]{1,0:T(8,128)(2,1)} custom-call(bf16[48,64,2,227]{3,2,1,0:T(2,128)(2,1)} %refs_0_.1, s32[128]{0:T(128)} %refs_1_.1, s32[1,128]{1,0:T(1,128)} %bitcast.17, s32[1,256]{1,0:T(1,128)} %bitcast.15, s32[1,256]{1,0:T(1,128)} %bitcast.16, bf16[32,512]{1,0:T(8,128)(2,1)} %refs_5_.1, bf16[128,512]{1,0:T(8,128)(2,1)} %refs_6_.1, ...), custom_call_target="tpu_custom_call" | custom-call | flops 4000000000 | bytes 15000000 | tf_op jit(solution)/shard_map/pallas_call | solution.py:544
  41.2 1.5 %reshape.39 = bf16[32,2,512]{2,1,0:T(2,128)(2,1)} reshape(bf16[64,512]{1,0:T(8,128)(2,1)} %shard_map.262) | data formatting | bytes 131072 | tf_op jit(solution)/shard_map/reshape | solution.py:556

commit v6 on v4

--- a/solution.py
+++ b/solution.py
@@ -26,6 +26,7 @@
 NEAR = (1, 15, 16, 17, 31, 112, 113, 127)
 EXTRA = 3
 SLOTS = PAIRS + EXTRA * len(NEAR)
+CLOSE = 4 * NODES + 2 * EXTRA * len(NEAR)
 DIRECTIONS = tuple((a, b) for a in (0, -1, 1) for b in (0, -1, 1) if (a, b) != (0, 0))
 
 
@@ -61,6 +62,7 @@
 
 
 class Held(NamedTuple):
+    g2m_sender: Any
     g2m_receiver: Any
     mesh_sender: Any
     mesh_receiver: Any
@@ -90,6 +92,8 @@
 
 
 FETCHED = len(Held._fields)
+FIRST = FETCHED - 9
+PIECES = 4
 
 
 def mm(a, b):
@@ -145,16 +149,17 @@
 
 
 def kernel(*refs):
-    grid_hbm, sender_hbm = refs[:2]
-    hbm = refs[2 : 2 + FETCHED]
-    out_ref = refs[2 + FETCHED]
-    refs = refs[3 + FETCHED :]
+    grid_hbm = refs[0]
+    hbm = refs[1 : 1 + FETCHED]
+    out_ref = refs[1 + FETCHED]
+    refs = refs[2 + FETCHED :]
     held = Held(*refs[:FETCHED])
     (
-        cells, sender, picked, pick_all, gather_far, gather_own, gather_recv, edge_base,
+        cells, found, sender, picked, pick_all, gather_far, gather_close, close_rows, edge_base,
         req_out, req_in, out_rows, in_rows,
         fetch_sem, cells_sem, sender_sem,
         halo_send, halo_recv, req_send, req_recv, row_send, row_recv,
+        more_send, more_recv,
     ) = refs[FETCHED:]
 
     lat = lax.axis_index("lat")
@@ -178,12 +183,39 @@
 
         lax.fori_loop(1, LATS, band, 0)
 
+    fetches = [
+        pltpu.make_async_copy(hbm[n], held[n], fetch_sem.at[n]) for n in range(FETCHED)
+    ]
+    fetch = Held(*fetches)
+
+    def ready(*copies):
+        for copy in copies:
+            copy.wait()
+
+    for copy in fetches[:4]:
+        copy.start()
+    cells_copies = []
+    for n in range(PIECES):
+        rows = lat_rows // PIECES
+        cells_copies.append(
+            pltpu.make_async_copy(
+                grid_hbm.at[pl.ds(n * rows, rows)],
+                cells.at[pl.ds(HALO + n * rows, rows), pl.ds(HALO, lon_cols)],
+                cells_sem.at[n],
+            )
+        )
+    for copy in cells_copies:
+        copy.start()
+
     barrier = pltpu.get_barrier_semaphore()
     for i in NEAR:
         pl.semaphore_signal(
             barrier, inc=1, device_id=place(i // LONS, i % LONS, 1), device_id_type=MESH
         )
 
+    for copy in fetches[4:FIRST]:
+        copy.start()
+
     def greet(step_lat, step_lon):
         pl.semaphore_signal(
             barrier, inc=1, device_id=place(step_lat, step_lon, 1), device_id_type=MESH
@@ -200,27 +232,14 @@
 
     lax.fori_loop(2, LATS - 1, greet_band, 0)
 
-    sender_copy = pltpu.make_async_copy(sender_hbm, sender, sender_sem)
+    ready(fetch.g2m_sender, fetch.g2m_receiver, fetch.mesh_sender, fetch.mesh_receiver)
+    cell = held.g2m_sender[...]
+    cell_row = (cell >> 10) - lat * lat_rows + HALO
+    cell_col = ((cell & (LONS * lon_cols - 1)) - lon * lon_cols + HALO) & (LONS * lon_cols - 1)
+    found[0:1] = jnp.clip(cell_row, 0, cells.shape[0] - 1)
+    found[1:2] = jnp.clip(cell_col, 0, cells.shape[1] - 1)
+    sender_copy = pltpu.make_async_copy(found, sender, sender_sem)
     sender_copy.start()
-    fetches = [
-        pltpu.make_async_copy(hbm[n], held[n], fetch_sem.at[n]) for n in range(FETCHED)
-    ]
-    fetch = Held(*fetches)
-
-    def ready(*copies):
-        for copy in copies:
-            copy.wait()
-
-    for copy in fetches[:3]:
-        copy.start()
-    cells_copy = pltpu.make_async_copy(
-        grid_hbm, cells.at[pl.ds(HALO, lat_rows), pl.ds(HALO, lon_cols)], cells_sem
-    )
-    cells_copy.start()
-    for copy in fetches[3:]:
-        copy.start()
-
-    ready(fetch.g2m_receiver, fetch.mesh_sender, fetch.mesh_receiver)
     senders = held.mesh_sender[...]
     owner = senders >> 5
     row = senders & (NODES - 1)
@@ -284,6 +303,9 @@
 
     for_all_others(ask)
 
+    for copy in fetches[FIRST:]:
+        copy.start()
+
     grid_receivers = held.g2m_receiver[...]
     shape = (2 * NODES, 2 * GRID_EDGES)
     total_grid = hot(
@@ -306,7 +328,8 @@
     state = mm(hot(iota(shape, 1) == (iota(shape, 0) >> 1)), latents).astype(BF)
 
     sender_copy.wait()
-    cells_copy.wait()
+    for copy in cells_copies:
+        copy.wait()
     for copy in groups[0]:
         copy.wait_recv()
 
@@ -320,18 +343,11 @@
         for copy in groups[2]:
             copy.wait_recv()
 
-    width = lon_cols * LONS
-
     def pick(k, carry):
-        cell = sender[k]
-        cell_row = (cell >> 10) - lat * lat_rows + HALO
-        cell_col = ((cell & (width - 1)) - lon * lon_cols + HALO + width) & (width - 1)
-        cell_row = jnp.clip(cell_row, 0, cells.shape[0] - 1)
-        cell_col = jnp.clip(cell_col, 0, cells.shape[1] - 1)
-        picked[k] = cells[cell_row, cell_col]
+        picked[k] = cells[sender[0, k], sender[1, k]]
         return carry
 
-    lax.fori_loop(0, GRID_EDGES, pick, 0, unroll=16)
+    lax.fori_loop(0, GRID_EDGES, pick, 0, unroll=32)
 
     ready(fetch.embed_w1, fetch.embed_b1, fetch.embed_w2, fetch.embed_gain)
     inputs = picked[...].reshape(2 * GRID_EDGES, picked.shape[2])
@@ -383,6 +399,14 @@
         outgoing = mm(state, held.proc_edge_w1[t, 1]).astype(BF)
         out_rows[t] = mm(pick_all[...], outgoing).astype(BF).reshape(SLOTS, 2, D)
 
+        for n, i in enumerate(NEAR):
+            span = pl.ds(PAIRS + EXTRA * n, EXTRA)
+            pltpu.make_async_remote_copy(
+                src_ref=out_rows.at[t, span], dst_ref=in_rows.at[t, span],
+                send_sem=more_send.at[t], recv_sem=more_recv.at[t],
+                device_id=place(i // LONS, i % LONS, -1), device_id_type=MESH,
+            ).start()
+
         def give(step_lat, step_lon, t=t):
             i = step_lat * LONS + step_lon
             pltpu.make_async_remote_copy(
@@ -392,13 +416,6 @@
             ).start()
 
         for_all_others(give)
-        for n, i in enumerate(NEAR):
-            span = pl.ds(PAIRS + EXTRA * n, EXTRA)
-            pltpu.make_async_remote_copy(
-                src_ref=out_rows.at[t, span], dst_ref=in_rows.at[t, span],
-                send_sem=row_send.at[t], recv_sem=row_recv.at[t],
-                device_id=place(i // LONS, i % LONS, -1), device_id_type=MESH,
-            ).start()
 
         if t == 0:
             owner1 = hot(iota((PAIRS, EDGES), 0) == rel)
@@ -410,17 +427,20 @@
             near = jnp.zeros_like(rel)
             for n, i in enumerate(NEAR):
                 near = jnp.where(rel == i, n, near)
-            slot = jnp.where(rank == 0, rel, PAIRS + EXTRA * near + rank - 1)
-            slot = jnp.where(rel == 0, SLOTS + row, slot)
-            slot_column = doubled_column(slot, EDGES)
-            shape = (2 * EDGES, 2 * (SLOTS + NODES))
-            gather = hot(iota(shape, 1) == 2 * slot_column + (iota(shape, 0) & 1))
-            gather_far[...] = gather[:, : 2 * SLOTS]
-            gather_own[...] = gather[:, 2 * SLOTS :]
+            nowhere = -PAIRS
+            far = jnp.where((rank == 0) & (rel > 0), rel, nowhere)
+            close = jnp.where(rank == 0, nowhere, 2 * NODES + EXTRA * near + rank - 1)
+            close = jnp.where(rel == 0, NODES + row, close)
+            shape = (2 * EDGES, 2 * PAIRS)
+            gather_far[...] = hot(
+                iota(shape, 1) == 2 * doubled_column(far, EDGES) + (iota(shape, 0) & 1)
+            )
             receivers = held.mesh_receiver[...]
-            shape = (2 * EDGES, 2 * NODES)
-            gather_recv[...] = hot(
-                iota(shape, 1) == 2 * doubled_column(receivers, EDGES) + (iota(shape, 0) & 1)
+            shape = (2 * EDGES, CLOSE)
+            lane = iota(shape, 1) - (iota(shape, 0) & 1)
+            gather_close[...] = hot(
+                (lane == 2 * doubled_column(receivers, EDGES))
+                | (lane == 2 * doubled_column(close, EDGES))
             )
             shape = (2 * NODES, 2 * EDGES)
             total_mesh = hot(iota(shape, 0) == 2 * doubled_row(receivers, EDGES) + (iota(shape, 1) & 1))
@@ -431,18 +451,21 @@
                 hot(iota(shape, 1) == (iota(shape, 0) >> 1)), held.mesh_edges[...]
             ).astype(BF)
 
-        incoming = mm(state, held.proc_edge_w1[t, 2]).astype(BF)
+        close_rows[: 2 * NODES] = mm(state, held.proc_edge_w1[t, 2]).astype(BF)
+        close_rows[2 * NODES : 4 * NODES] = outgoing
+        node_base = mm(state, held.proc_node_w1[t, 0]) + held.proc_node_b1[t : t + 1]
+        arrived = in_rows.at[t, pl.ds(PAIRS, SLOTS - PAIRS)]
+        pltpu.make_async_copy(arrived, arrived, more_recv.at[t]).wait()
+        close_rows[4 * NODES :] = in_rows[t, PAIRS:].reshape(2 * (SLOTS - PAIRS), D)
         edge_base[...] = (
             mm(edge_state, held.proc_edge_w1[t, 0])
-            + mm(gather_recv[...], incoming)
-            + mm(gather_own[...], outgoing)
+            + mm(gather_close[...], close_rows[...])
             + held.proc_edge_b1[t : t + 1]
         )
-        node_base = mm(state, held.proc_node_w1[t, 0]) + held.proc_node_b1[t : t + 1]
-
-        arrived = in_rows.at[t, pl.ds(1, SLOTS - 1)]
+
+        arrived = in_rows.at[t, pl.ds(1, PAIRS - 1)]
         pltpu.make_async_copy(arrived, arrived, row_recv.at[t]).wait()
-        table = in_rows[t].reshape(2 * SLOTS, D)
+        table = in_rows[t, :PAIRS].reshape(2 * PAIRS, D)
         gain = held.proc_edge_gain[t : t + 1]
         halves = []
         for span in (slice(0, EDGES), slice(EDGES, 2 * EDGES)):
@@ -472,8 +495,10 @@
     asked_all = req_out.at[pl.ds(1, PAIRS - 1)]
     pltpu.make_async_copy(asked_all, asked_all, req_send).wait()
     for t in range(STEPS):
-        sent = out_rows.at[t, pl.ds(1, SLOTS - 1)]
+        sent = out_rows.at[t, pl.ds(1, PAIRS - 1)]
         pltpu.make_async_copy(sent, sent, row_send.at[t]).wait()
+        sent = out_rows.at[t, pl.ds(PAIRS, SLOTS - PAIRS)]
+        pltpu.make_async_copy(sent, sent, more_send.at[t]).wait()
 
 
 def on_device(*args):
@@ -484,6 +509,7 @@
         return row.reshape(1, row.shape[0])
 
     wanted = Held(
+        flat(given.g2m_sender),
         flat(given.g2m_receiver),
         flat(given.mesh_sender),
         flat(given.mesh_receiver),
@@ -511,29 +537,32 @@
         given.proc_node_w2,
         given.proc_node_gain,
     )
-    operands = [given.grid_inputs, given.g2m_sender, *wanted]
+    operands = [given.grid_inputs, *wanted]
     dma = pltpu.SemaphoreType.DMA
     scratch = [pltpu.VMEM(part.shape, part.dtype) for part in wanted]
     scratch += [
         pltpu.VMEM((lat_rows + 2 * HALO, lon_cols + 2 * HALO, batch, width), BF),
-        pltpu.SMEM((GRID_EDGES,), I32),
+        pltpu.VMEM((2, GRID_EDGES), I32),
+        pltpu.SMEM((2, GRID_EDGES), I32),
         pltpu.VMEM((GRID_EDGES, batch, width), BF),
         pltpu.VMEM((2 * SLOTS, 2 * NODES), BF),
-        pltpu.VMEM((2 * EDGES, 2 * SLOTS), BF),
-        pltpu.VMEM((2 * EDGES, 2 * NODES), BF),
-        pltpu.VMEM((2 * EDGES, 2 * NODES), BF),
+        pltpu.VMEM((2 * EDGES, 2 * PAIRS), BF),
+        pltpu.VMEM((2 * EDGES, CLOSE), BF),
+        pltpu.VMEM((CLOSE, D), BF),
         pltpu.VMEM((2 * EDGES, D), F32),
         pltpu.VMEM((PAIRS, 2, 128), BF),
         pltpu.VMEM((PAIRS, 2, 128), BF),
         pltpu.VMEM((STEPS, SLOTS, 2, D), BF),
         pltpu.VMEM((STEPS, SLOTS, 2, D), BF),
         dma((FETCHED,)),
-        dma,
+        dma((PIECES,)),
         dma,
         dma((len(DIRECTIONS),)),
         dma((len(DIRECTIONS),)),
         dma,
         dma,
+        dma((STEPS,)),
+        dma((STEPS,)),
         dma((STEPS,)),
         dma((STEPS,)),
     ]

time: 42.2 us -> 41.6 us (0.986)
  Pallas kernels: 40.5 us -> 39.9 us
    pallas_call x1, Pallas kernels: 40.5 us -> 39.9 us  [on_device(): pl.pallas_call(kernel, out_shape=jax.ShapeDtypeStruct((NODES * batch, D),...]
where the time goes in v6:
time: 41.6 us; the launch traced here: 41.4 us
  Pallas kernels  39.9 us (96%)
  local copies, waits for them, and re-layouts  1.5 us (4%)
    pallas_call x1, Pallas kernels, on_device(): pl.pallas_call(kernel, out_shape=jax.ShapeDtypeStruct((NODES * batch, D),...  39.9 us
    reshape x1, local copies, waits for them, and re-layouts, on_device(): return pl.pallas_call(kernel, out_shape=jax.ShapeDtypeStruct((NODES * bat...  1.5 us

profile of v6, /device:TPU:1, one launch (start us, length us, event | category | flops | bytes accessed | tf_op | source)
XLA Modules:
  0.0 41.4 jit_solution(7093475917302945237)
XLA Ops:
  0.0 39.9 %shard_map.262 = bf16[64,512]{1,0:T(8,128)(2,1)} custom-call(bf16[48,64,2,227]{3,2,1,0:T(2,128)(2,1)} %refs_0_.1, s32[1,128]{1,0:T(1,128)} %bitcast.18, s32[1,128]{1,0:T(1,128)} %bitcast.19, s32[1,256]{1,0:T(1,128)} %bitcast.16, s32[1,256]{1,0:T(1,128)} %bitcast.17, bf16[32,512]{1,0:T(8,128)(2,1)} %refs_5_.1, bf16[128,512]{1,0:T(8,128)(2,1)} %refs_6_.1, ...), custom_call_target="tpu_custom_call" | custom-call | flops 4000000000 | bytes 15000000 | tf_op jit(solution)/shard_map/pallas_call | solution.py:569
  39.9 1.5 %reshape.43 = bf16[32,2,512]{2,1,0:T(2,128)(2,1)} reshape(bf16[64,512]{1,0:T(8,128)(2,1)} %shard_map.262) | data formatting | bytes 131072 | tf_op jit(solution)/shard_map/reshape | solution.py:581

commit v7 on v3

--- a/solution.py
+++ b/solution.py
@@ -16,6 +16,7 @@
 D = 512
 HALO = 2
 STEPS = 2
+CHUNK = 64
 LATS = 8
 LONS = 16
 CORES = 2
@@ -30,6 +31,7 @@
 EXTRA = (6, 6, 3, 3, 3, 3, 3, 3)
 START = (0, 6, 12, 15, 18, 21, 24, 27)
 SLOTS = PLAIN + sum(EXTRA)
+CLOSE = 2 * NODES + 2 * CHIP_NODES + 2 * sum(EXTRA)
 DIRECTIONS = tuple((a, b) for a in (0, -1, 1) for b in (0, -1, 1) if (a, b) != (0, 0))
 
 
@@ -65,6 +67,7 @@
 
 
 class Held(NamedTuple):
+    g2m_sender: Any
     g2m_receiver: Any
     mesh_sender: Any
     mesh_receiver: Any
@@ -94,6 +97,8 @@
 
 
 FETCHED = len(Held._fields)
+FIRST = FETCHED - 9
+PIECES = 4
 
 
 def mm(a, b):
@@ -123,6 +128,20 @@
     return centered * lax.rsqrt(variance + 1e-05) * gain
 
 
+def by_rows(act, *arrays):
+    count = arrays[0].shape[0]
+    pieces = [act(*(v[c : c + CHUNK] for v in arrays)) for c in range(0, count, CHUNK)]
+    return jnp.concatenate(pieces, axis=0)
+
+
+def silu_rows(*terms):
+    return by_rows(lambda *parts: silu(sum(parts[1:], parts[0])).astype(BF), *terms)
+
+
+def updated_rows(rows, v, gain):
+    return by_rows(lambda r, part: (r.astype(F32) + norm(part, gain)).astype(BF), rows, v)
+
+
 def doubled_column(row, count):
     shape = (2 * count, count)
     spread = jnp.where(iota(shape, 1) == (iota(shape, 0) >> 1), row.astype(F32), 0.0)
@@ -135,17 +154,17 @@
 
 
 def kernel(*refs):
-    grid_hbm, sender_hbm = refs[:2]
-    hbm = refs[2 : 2 + FETCHED]
-    out_ref = refs[2 + FETCHED]
-    refs = refs[3 + FETCHED :]
+    grid_hbm = refs[0]
+    hbm = refs[1 : 1 + FETCHED]
+    out_ref = refs[1 + FETCHED]
+    refs = refs[2 + FETCHED :]
     held = Held(*refs[:FETCHED])
     (
-        cells, sender, picked, pick_all, gather_far, gather_own, gather_recv, edge_base,
+        cells, found, sender, picked, pick_all, gather_far, gather_close, close_rows, edge_base,
         req_out, req_in, chip_rows, out_rows, in_rows,
         fetch_sem, cells_sem, sender_sem,
-        halo_send, halo_recv, req_send, req_recv, share_send, share_recv,
-        row_send, row_recv,
+        halo_send, halo_recv, req_send, req_recv, row_send, row_recv,
+        more_send, more_recv, share_send, share_recv,
     ) = refs[FETCHED:]
 
     lat = lax.axis_index("lat")
@@ -172,35 +191,64 @@
 
         lax.fori_loop(1, XS, band, 0)
 
+    fetches = [
+        pltpu.make_async_copy(hbm[n], held[n], fetch_sem.at[n]) for n in range(FETCHED)
+    ]
+    fetch = Held(*fetches)
+
+    def ready(*copies):
+        for copy in copies:
+            copy.wait()
+
+    for copy in fetches[:4]:
+        copy.start()
+    cells_copies = []
+    for n in range(PIECES):
+        rows = lat_rows // PIECES
+        cells_copies.append(
+            pltpu.make_async_copy(
+                grid_hbm.at[pl.ds(n * rows, rows)],
+                cells.at[pl.ds(HALO + n * rows, rows), pl.ds(HALO, lon_cols)],
+                cells_sem.at[n],
+            )
+        )
+    for copy in cells_copies:
+        copy.start()
+
     barrier = pltpu.get_barrier_semaphore()
     others = [(a, b) for a in (-1, 1) for b in (0, -1, 1)]
-    for a, b in others:
+    for a, b in others + [(0, -1), (0, 1)]:
         pl.semaphore_signal(
             barrier, inc=1, device_id_type=MESH,
             device_id=((lat + a + LATS) & (LATS - 1), (lon + b + LONS) & (LONS - 1)),
         )
 
+    for copy in fetches[4:FIRST]:
+        copy.start()
+
     def greet(step_x, step_lon):
         pl.semaphore_signal(
             barrier, inc=1, device_id=place(step_x, step_lon, 1), device_id_type=MESH
         )
 
-    for_all_chips(greet)
-
-    sender_copy = pltpu.make_async_copy(sender_hbm, sender, sender_sem)
+    for step_lon in range(2, LONS - 1):
+        greet(0, step_lon)
+
+    def greet_band(step_x, carry):
+        for step_lon in range(LONS):
+            greet(step_x, step_lon)
+        return carry
+
+    lax.fori_loop(1, XS, greet_band, 0)
+
+    ready(fetch.g2m_sender, fetch.g2m_receiver, fetch.mesh_sender, fetch.mesh_receiver)
+    cell = held.g2m_sender[...]
+    cell_row = (cell >> 10) - lat * lat_rows + HALO
+    cell_col = ((cell & (LONS * lon_cols - 1)) - lon * lon_cols + HALO) & (LONS * lon_cols - 1)
+    found[0:1] = jnp.clip(cell_row, 0, cells.shape[0] - 1)
+    found[1:2] = jnp.clip(cell_col, 0, cells.shape[1] - 1)
+    sender_copy = pltpu.make_async_copy(found, sender, sender_sem)
     sender_copy.start()
-    fetches = [
-        pltpu.make_async_copy(hbm[n], held[n], fetch_sem.at[n]) for n in range(FETCHED)
-    ]
-    fetch = Held(*fetches)
-
-    def ready(*copies):
-        for copy in copies:
-            copy.wait()
-
-    for copy in fetches[:3]:
-        copy.start()
-    ready(fetch.g2m_receiver, fetch.mesh_sender, fetch.mesh_receiver)
     senders = held.mesh_sender[...]
     owner = senders >> 5
     step_x = ((owner >> 5) - (lat >> 1)) & (XS - 1)
@@ -257,13 +305,6 @@
         for copy in groups[2]:
             copy.start()
 
-    cells_copy = pltpu.make_async_copy(
-        grid_hbm, cells.at[pl.ds(HALO, lat_rows), pl.ds(HALO, lon_cols)], cells_sem
-    )
-    cells_copy.start()
-    for copy in fetches[3:]:
-        copy.start()
-
     def ask(step_x, step_lon):
         i = step_x * LONS + step_lon
         pltpu.make_async_remote_copy(
@@ -272,6 +313,9 @@
         ).start()
 
     for_all_chips(ask)
+
+    for copy in fetches[FIRST:]:
+        copy.start()
 
     grid_receivers = held.g2m_receiver[...]
     shape = (2 * NODES, 2 * GRID_EDGES)
@@ -295,7 +339,8 @@
     state = mm(hot(iota(shape, 1) == (iota(shape, 0) >> 1)), latents).astype(BF)
 
     sender_copy.wait()
-    cells_copy.wait()
+    for copy in cells_copies:
+        copy.wait()
     for copy in groups[0]:
         copy.wait_recv()
 
@@ -309,25 +354,19 @@
         for copy in groups[2]:
             copy.wait_recv()
 
-    width = lon_cols * LONS
-
     def pick(k, carry):
-        cell = sender[k]
-        cell_row = (cell // width) - lat * lat_rows + HALO
-        cell_col = ((cell & (width - 1)) - lon * lon_cols + HALO + width) & (width - 1)
-        cell_row = jnp.clip(cell_row, 0, cells.shape[0] - 1)
-        cell_col = jnp.clip(cell_col, 0, cells.shape[1] - 1)
-        picked[k] = cells[cell_row, cell_col]
+        picked[k] = cells[sender[0, k], sender[1, k]]
         return carry
 
-    lax.fori_loop(0, GRID_EDGES, pick, 0, unroll=8)
+    lax.fori_loop(0, GRID_EDGES, pick, 0, unroll=32)
 
     ready(fetch.embed_w1, fetch.embed_b1, fetch.embed_w2, fetch.embed_gain)
     inputs = picked[...].reshape(2 * GRID_EDGES, picked.shape[2])
-    hidden = silu(mm(inputs, held.embed_w1[...]) + held.embed_b1[...]).astype(BF)
-    latent = norm(mm(hidden, held.embed_w2[...]), held.embed_gain[...]).astype(BF)
-    preact = mm(latent, held.enc_edge_w1[1]) + grid_base
-    hidden = silu(preact).astype(BF)
+    bias = held.embed_b1[...]
+    hidden = by_rows(lambda v: silu(v + bias).astype(BF), mm(inputs, held.embed_w1[...]))
+    gain = held.embed_gain[...]
+    latent = by_rows(lambda v: norm(v, gain).astype(BF), mm(hidden, held.embed_w2[...]))
+    hidden = silu_rows(mm(latent, held.enc_edge_w1[1]), grid_base)
     asked_all = req_in.at[pl.ds(1, CHIPS - 1)]
     pltpu.make_async_copy(asked_all, asked_all, req_recv).wait()
     wanted = req_in[...].reshape(2 * CHIPS, 2 * CHIP_NODES)
@@ -350,8 +389,7 @@
     pick_all[...] = jnp.where(mm(choose, place_of) == kth, mm(choose, wanted), 0.0).astype(BF)
 
     ready(fetch.enc_edge_w2, fetch.enc_edge_gain)
-    update = norm(mm(hidden, held.enc_edge_w2[...]), held.enc_edge_gain[...])
-    new_edges = (grid_edges.astype(F32) + update).astype(BF)
+    new_edges = updated_rows(grid_edges, mm(hidden, held.enc_edge_w2[...]), held.enc_edge_gain[...])
     summed = mm(total_grid, new_edges).astype(BF)
     ready(fetch.enc_node_w1, fetch.enc_node_b1, fetch.enc_node_w2, fetch.enc_node_gain)
     preact = (
@@ -373,7 +411,7 @@
             device_id=(beside, lon), device_id_type=MESH,
         )
         share.start()
-        incoming = mm(state, held.proc_edge_w1[t, 2]).astype(BF)
+        close_rows[: 2 * NODES] = mm(state, held.proc_edge_w1[t, 2]).astype(BF)
         node_base = mm(state, held.proc_node_w1[t, 0]) + held.proc_node_b1[t : t + 1]
         share.wait()
         outgoing = chip_rows[t].reshape(2 * CHIP_NODES, D)
@@ -383,7 +421,7 @@
             span = pl.ds(PLAIN + START[n], EXTRA[n])
             pltpu.make_async_remote_copy(
                 src_ref=out_rows.at[t, span], dst_ref=in_rows.at[t, span],
-                send_sem=row_send.at[t], recv_sem=row_recv.at[t],
+                send_sem=more_send.at[t], recv_sem=more_recv.at[t],
                 device_id=place(i // LONS, i % LONS, -1), device_id_type=MESH,
             ).start()
 
@@ -408,17 +446,21 @@
             extra = jnp.zeros_like(rel)
             for i, start in zip(NEAR, START):
                 extra = jnp.where(rel == i, start, extra)
-            slot = jnp.where(rank < 2, 2 * rel + rank, PLAIN + extra + rank - 2)
-            slot = jnp.where(rel == 0, SLOTS + row, slot)
-            slot_column = doubled_column(slot, EDGES)
-            shape = (2 * EDGES, 2 * (SLOTS + CHIP_NODES))
-            gather = hot(iota(shape, 1) == 2 * slot_column + (iota(shape, 0) & 1))
-            gather_far[...] = gather[:, : 2 * SLOTS]
-            gather_own[...] = gather[:, 2 * SLOTS :]
+            nowhere = -PLAIN
+            far = jnp.where((rank < 2) & (rel > 0), 2 * rel + rank, nowhere)
+            close = NODES + CHIP_NODES + extra + rank - 2
+            close = jnp.where(rank < 2, nowhere, close)
+            close = jnp.where(rel == 0, NODES + row, close)
+            shape = (2 * EDGES, 2 * PLAIN)
+            gather_far[...] = hot(
+                iota(shape, 1) == 2 * doubled_column(far, EDGES) + (iota(shape, 0) & 1)
+            )
             receivers = held.mesh_receiver[...]
-            shape = (2 * EDGES, 2 * NODES)
-            gather_recv[...] = hot(
-                iota(shape, 1) == 2 * doubled_column(receivers, EDGES) + (iota(shape, 0) & 1)
+            shape = (2 * EDGES, CLOSE)
+            lane = iota(shape, 1) - (iota(shape, 0) & 1)
+            gather_close[...] = hot(
+                (lane == 2 * doubled_column(receivers, EDGES))
+                | (lane == 2 * doubled_column(close, EDGES))
             )
             shape = (2 * NODES, 2 * EDGES)
             total_mesh = hot(iota(shape, 0) == 2 * doubled_row(receivers, EDGES) + (iota(shape, 1) & 1))
@@ -429,18 +471,26 @@
                 hot(iota(shape, 1) == (iota(shape, 0) >> 1)), held.mesh_edges[...]
             ).astype(BF)
 
+        own_end = 2 * (NODES + CHIP_NODES)
+        close_rows[2 * NODES : own_end] = outgoing
+        arrived = in_rows.at[t, pl.ds(PLAIN, SLOTS - PLAIN)]
+        pltpu.make_async_copy(arrived, arrived, more_recv.at[t]).wait()
+        close_rows[own_end:] = in_rows[t, PLAIN:].reshape(2 * (SLOTS - PLAIN), D)
         edge_base[...] = (
             mm(edge_state, held.proc_edge_w1[t, 0])
-            + mm(gather_recv[...], incoming)
-            + mm(gather_own[...], outgoing)
+            + mm(gather_close[...], close_rows[...])
             + held.proc_edge_b1[t : t + 1]
         )
-        arrived = in_rows.at[t, pl.ds(2, SLOTS - 2)]
+
+        arrived = in_rows.at[t, pl.ds(2, PLAIN - 2)]
         pltpu.make_async_copy(arrived, arrived, row_recv.at[t]).wait()
-        table = in_rows[t].reshape(2 * SLOTS, D)
-        hidden = silu(edge_base[...] + mm(gather_far[...], table)).astype(BF)
-        update = norm(mm(hidden, held.proc_edge_w2[t]), held.proc_edge_gain[t : t + 1])
-        edge_state = (edge_state.astype(F32) + update).astype(BF)
+        table = in_rows[t, :PLAIN].reshape(2 * PLAIN, D)
+        gain = held.proc_edge_gain[t : t + 1]
+        halves = []
+        for span in (slice(0, EDGES), slice(EDGES, 2 * EDGES)):
+            hidden = silu_rows(mm(gather_far[span], table), edge_base[span])
+            halves.append(updated_rows(edge_state[span], mm(hidden, held.proc_edge_w2[t]), gain))
+        edge_state = jnp.concatenate(halves, axis=0)
         summed = mm(total_mesh, edge_state).astype(BF)
         hidden = silu(node_base + mm(summed, held.proc_node_w1[t, 1])).astype(BF)
         update = norm(mm(hidden, held.proc_node_w2[t]), held.proc_node_gain[t : t + 1])
@@ -464,8 +514,10 @@
     asked_all = req_out.at[pl.ds(1, CHIPS - 1)]
     pltpu.make_async_copy(asked_all, asked_all, req_send).wait()
     for t in range(STEPS):
-        sent = out_rows.at[t, pl.ds(2, SLOTS - 2)]
+        sent = out_rows.at[t, pl.ds(2, PLAIN - 2)]
         pltpu.make_async_copy(sent, sent, row_send.at[t]).wait()
+        sent = out_rows.at[t, pl.ds(PLAIN, SLOTS - PLAIN)]
+        pltpu.make_async_copy(sent, sent, more_send.at[t]).wait()
 
 
 def on_device(*args):
@@ -476,6 +528,7 @@
         return row.reshape(1, row.shape[0])
 
     wanted = Held(
+        flat(given.g2m_sender),
         flat(given.g2m_receiver),
         flat(given.mesh_sender),
         flat(given.mesh_receiver),
@@ -503,17 +556,18 @@
         given.proc_node_w2,
         given.proc_node_gain,
     )
-    operands = [given.grid_inputs, given.g2m_sender, *wanted]
+    operands = [given.grid_inputs, *wanted]
     dma = pltpu.SemaphoreType.DMA
     scratch = [pltpu.VMEM(part.shape, part.dtype) for part in wanted]
     scratch += [
         pltpu.VMEM((lat_rows + 2 * HALO, lon_cols + 2 * HALO, batch, width), BF),
-        pltpu.SMEM((GRID_EDGES,), I32),
+        pltpu.VMEM((2, GRID_EDGES), I32),
+        pltpu.SMEM((2, GRID_EDGES), I32),
         pltpu.VMEM((GRID_EDGES, batch, width), BF),
         pltpu.VMEM((2 * SLOTS, 2 * CHIP_NODES), BF),
-        pltpu.VMEM((2 * EDGES, 2 * SLOTS), BF),
-        pltpu.VMEM((2 * EDGES, 2 * CHIP_NODES), BF),
-        pltpu.VMEM((2 * EDGES, 2 * NODES), BF),
+        pltpu.VMEM((2 * EDGES, 2 * PLAIN), BF),
+        pltpu.VMEM((2 * EDGES, CLOSE), BF),
+        pltpu.VMEM((CLOSE, D), BF),
         pltpu.VMEM((2 * EDGES, D), F32),
         pltpu.VMEM((CHIPS, 2, 2 * CHIP_NODES), BF),
         pltpu.VMEM((CHIPS, 2, 2 * CHIP_NODES), BF),
@@ -521,12 +575,14 @@
         pltpu.VMEM((STEPS, SLOTS, 2, D), BF),
         pltpu.VMEM((STEPS, SLOTS, 2, D), BF),
         dma((FETCHED,)),
-        dma,
+        dma((PIECES,)),
         dma,
         dma((len(DIRECTIONS),)),
         dma((len(DIRECTIONS),)),
         dma,
         dma,
+        dma((STEPS,)),
+        dma((STEPS,)),
         dma((STEPS,)),
         dma((STEPS,)),
         dma((STEPS,)),

time: 44.5 us -> 43.4 us (0.975)
  Pallas kernels: 42.8 us -> 41.8 us
    pallas_call x1, Pallas kernels: 42.8 us -> 41.8 us  [on_device(): pl.pallas_call(kernel, out_shape=jax.ShapeDtypeStruct((NODES * batch, D),...]
where the time goes in v7:
time: 43.4 us; the launch traced here: 43.3 us
  Pallas kernels  41.8 us (96%)
  local copies, waits for them, and re-layouts  1.5 us (3%)
    pallas_call x1, Pallas kernels, on_device(): pl.pallas_call(kernel, out_shape=jax.ShapeDtypeStruct((NODES * batch, D),...  41.8 us
    reshape x1, local copies, waits for them, and re-layouts, on_device(): return pl.pallas_call(kernel, out_shape=jax.ShapeDtypeStruct((NODES * bat...  1.5 us

profile of v7, /device:TPU:1, one launch (start us, length us, event | category | flops | bytes accessed | tf_op | source)
XLA Modules:
  0.0 43.3 jit_solution(12527803146222646681)
XLA Ops:
  0.0 41.8 %shard_map.262 = bf16[64,512]{1,0:T(8,128)(2,1)} custom-call(bf16[48,64,2,227]{3,2,1,0:T(2,128)(2,1)} %refs_0_.1, s32[1,128]{1,0:T(1,128)} %bitcast.18, s32[1,128]{1,0:T(1,128)} %bitcast.19, s32[1,256]{1,0:T(1,128)} %bitcast.16, s32[1,256]{1,0:T(1,128)} %bitcast.17, bf16[32,512]{1,0:T(8,128)(2,1)} %refs_5_.1, bf16[128,512]{1,0:T(8,128)(2,1)} %refs_6_.1, ...), custom_call_target="tpu_custom_call" | custom-call | flops 4000000000 | bytes 15000000 | tf_op jit(solution)/shard_map/pallas_call | solution.py:591
  41.8 1.5 %reshape.43 = bf16[32,2,512]{2,1,0:T(2,128)(2,1)} reshape(bf16[64,512]{1,0:T(8,128)(2,1)} %shard_map.262) | data formatting | bytes 131072 | tf_op jit(solution)/shard_map/reshape | solution.py:603

commit v8 on v6

--- a/solution.py
+++ b/solution.py
@@ -118,9 +118,11 @@
 
 
 def norm(v, gain):
-    centered = v - jnp.mean(v, axis=-1, keepdims=True)
-    variance = jnp.mean(centered * centered, axis=-1, keepdims=True)
-    return centered * lax.rsqrt(variance + 1e-05) * gain
+    count = 1.0 / v.shape[-1]
+    mean = jnp.sum(v, axis=-1, keepdims=True) * count
+    square = jnp.sum(v * v, axis=-1, keepdims=True) * count
+    scale = lax.rsqrt(jnp.maximum(square - mean * mean, 0.0) + 1e-05)
+    return (v - mean) * scale * gain
 
 
 def by_rows(act, *arrays):
@@ -327,6 +329,11 @@
     shape = (2 * NODES, NODES)
     state = mm(hot(iota(shape, 1) == (iota(shape, 0) >> 1)), latents).astype(BF)
 
+    ready(fetch.embed_w1, fetch.embed_b1, fetch.embed_w2, fetch.embed_gain)
+    ready(fetch.enc_edge_w2, fetch.enc_edge_gain)
+    ready(fetch.enc_node_w1, fetch.enc_node_b1, fetch.enc_node_w2, fetch.enc_node_gain)
+    enc_node_base = mm(state, held.enc_node_w1[0]) + held.enc_node_b1[...]
+
     sender_copy.wait()
     for copy in cells_copies:
         copy.wait()
@@ -349,7 +356,6 @@
 
     lax.fori_loop(0, GRID_EDGES, pick, 0, unroll=32)
 
-    ready(fetch.embed_w1, fetch.embed_b1, fetch.embed_w2, fetch.embed_gain)
     inputs = picked[...].reshape(2 * GRID_EDGES, picked.shape[2])
     bias = held.embed_b1[...]
     hidden = by_rows(lambda v: silu(v + bias).astype(BF), mm(inputs, held.embed_w1[...]))
@@ -380,21 +386,13 @@
     pick_all[: 2 * PAIRS] = first
     pick_all[2 * PAIRS :] = more
 
-    ready(fetch.enc_edge_w2, fetch.enc_edge_gain)
     new_edges = updated_rows(grid_edges, mm(hidden, held.enc_edge_w2[...]), held.enc_edge_gain[...])
     summed = mm(total_grid, new_edges).astype(BF)
-    ready(fetch.enc_node_w1, fetch.enc_node_b1, fetch.enc_node_w2, fetch.enc_node_gain)
-    preact = (
-        mm(state, held.enc_node_w1[0])
-        + mm(summed, held.enc_node_w1[1])
-        + held.enc_node_b1[...]
-    )
-    hidden = silu(preact).astype(BF)
+    hidden = silu(enc_node_base + mm(summed, held.enc_node_w1[1])).astype(BF)
     update = norm(mm(hidden, held.enc_node_w2[...]), held.enc_node_gain[...])
     state = (state.astype(F32) + update).astype(BF)
 
-    ready(fetch.proc_edge_w1, fetch.proc_edge_b1, fetch.proc_edge_w2, fetch.proc_edge_gain)
-    ready(fetch.proc_node_w1, fetch.proc_node_b1, fetch.proc_node_w2, fetch.proc_node_gain)
+    ready(fetch.proc_edge_w1)
     for t in range(STEPS):
         outgoing = mm(state, held.proc_edge_w1[t, 1]).astype(BF)
         out_rows[t] = mm(pick_all[...], outgoing).astype(BF).reshape(SLOTS, 2, D)
@@ -418,6 +416,8 @@
         for_all_others(give)
 
         if t == 0:
+            ready(fetch.proc_edge_b1, fetch.proc_edge_w2, fetch.proc_edge_gain)
+            ready(fetch.proc_node_w1, fetch.proc_node_b1, fetch.proc_node_w2, fetch.proc_node_gain)
             owner1 = hot(iota((PAIRS, EDGES), 0) == rel)
             row1 = iota((NODES, EDGES), 0) == row
             needed = hot(mm_nt(hot(row1), owner1) > 0.5)
@@ -472,7 +472,8 @@
             hidden = silu_rows(mm(gather_far[span], table), edge_base[span])
             halves.append(updated_rows(edge_state[span], mm(hidden, held.proc_edge_w2[t]), gain))
         edge_state = jnp.concatenate(halves, axis=0)
-        summed = mm(total_mesh, edge_state).astype(BF)
+        summed = mm(total_mesh[:, :EDGES], halves[0]) + mm(total_mesh[:, EDGES:], halves[1])
+        summed = summed.astype(BF)
         hidden = silu(node_base + mm(summed, held.proc_node_w1[t, 1])).astype(BF)
         update = norm(mm(hidden, held.proc_node_w2[t]), held.proc_node_gain[t : t + 1])
         state = (state.astype(F32) + update).astype(BF)

time: 41.6 us -> 40.8 us (0.981)
  Pallas kernels: 39.9 us -> 39.1 us
    pallas_call x1, Pallas kernels: 39.9 us -> 39.1 us  [on_device(): pl.pallas_call(kernel, out_shape=jax.ShapeDtypeStruct((NODES * batch, D),...]
where the time goes in v8:
time: 40.8 us; the launch traced here: 40.7 us
  Pallas kernels  39.1 us (96%)
  local copies, waits for them, and re-layouts  1.5 us (4%)
    pallas_call x1, Pallas kernels, on_device(): pl.pallas_call(kernel, out_shape=jax.ShapeDtypeStruct((NODES * batch, D),...  39.1 us
    reshape x1, local copies, waits for them, and re-layouts, on_device(): return pl.pallas_call(kernel, out_shape=jax.ShapeDtypeStruct((NODES * bat...  1.5 us

profile of v8, /device:TPU:1, one launch (start us, length us, event | category | flops | bytes accessed | tf_op | source)
XLA Modules:
  0.0 40.7 jit_solution(1686818198206039018)
XLA Ops:
  0.0 39.1 %shard_map.262 = bf16[64,512]{1,0:T(8,128)(2,1)} custom-call(bf16[48,64,2,227]{3,2,1,0:T(2,128)(2,1)} %refs_0_.1, s32[1,128]{1,0:T(1,128)} %bitcast.18, s32[1,128]{1,0:T(1,128)} %bitcast.19, s32[1,256]{1,0:T(1,128)} %bitcast.16, s32[1,256]{1,0:T(1,128)} %bitcast.17, bf16[32,512]{1,0:T(8,128)(2,1)} %refs_5_.1, bf16[128,512]{1,0:T(8,128)(2,1)} %refs_6_.1, ...), custom_call_target="tpu_custom_call" | custom-call | flops 4000000000 | bytes 15000000 | tf_op jit(solution)/shard_map/pallas_call | solution.py:570
  39.2 1.5 %reshape.43 = bf16[32,2,512]{2,1,0:T(2,128)(2,1)} reshape(bf16[64,512]{1,0:T(8,128)(2,1)} %shard_map.262) | data formatting | bytes 131072 | tf_op jit(solution)/shard_map/reshape | solution.py:582

commit v9 on v8

--- a/solution.py
+++ b/solution.py
@@ -215,9 +215,6 @@
             barrier, inc=1, device_id=place(i // LONS, i % LONS, 1), device_id_type=MESH
         )
 
-    for copy in fetches[4:FIRST]:
-        copy.start()
-
     def greet(step_lat, step_lon):
         pl.semaphore_signal(
             barrier, inc=1, device_id=place(step_lat, step_lon, 1), device_id_type=MESH
@@ -233,29 +230,6 @@
         return carry
 
     lax.fori_loop(2, LATS - 1, greet_band, 0)
-
-    ready(fetch.g2m_sender, fetch.g2m_receiver, fetch.mesh_sender, fetch.mesh_receiver)
-    cell = held.g2m_sender[...]
-    cell_row = (cell >> 10) - lat * lat_rows + HALO
-    cell_col = ((cell & (LONS * lon_cols - 1)) - lon * lon_cols + HALO) & (LONS * lon_cols - 1)
-    found[0:1] = jnp.clip(cell_row, 0, cells.shape[0] - 1)
-    found[1:2] = jnp.clip(cell_col, 0, cells.shape[1] - 1)
-    sender_copy = pltpu.make_async_copy(found, sender, sender_sem)
-    sender_copy.start()
-    senders = held.mesh_sender[...]
-    owner = senders >> 5
-    row = senders & (NODES - 1)
-    rel = ((((owner >> 4) - lat) & (LATS - 1)) << 4) | (((owner & 15) - lon) & (LONS - 1))
-    owner2 = hot((iota((2 * PAIRS, EDGES), 0) >> 1) == rel)
-    row2 = hot((iota((128, EDGES), 0) >> 1) == row)
-    asked = mm_nt(owner2, row2)
-    shape = (2 * PAIRS, 128)
-    same = (iota(shape, 0) & 1) == (iota(shape, 1) & 1)
-    asked = hot((asked > 0.5) & same & (iota(shape, 0) >= 2))
-    req_out[...] = asked.reshape(PAIRS, 2, 128)
-    req_in[0] = jnp.zeros((2, 128), BF)
-    for t in range(STEPS):
-        in_rows[t, 0] = jnp.zeros((2, D), BF)
 
     pl.semaphore_wait(barrier, PAIRS - 1)
 
@@ -295,6 +269,32 @@
     def _():
         for copy in groups[2]:
             copy.start()
+
+    for copy in fetches[4:FIRST]:
+        copy.start()
+
+    ready(fetch.g2m_sender, fetch.g2m_receiver, fetch.mesh_sender, fetch.mesh_receiver)
+    cell = held.g2m_sender[...]
+    cell_row = (cell >> 10) - lat * lat_rows + HALO
+    cell_col = ((cell & (LONS * lon_cols - 1)) - lon * lon_cols + HALO) & (LONS * lon_cols - 1)
+    found[0:1] = jnp.clip(cell_row, 0, cells.shape[0] - 1)
+    found[1:2] = jnp.clip(cell_col, 0, cells.shape[1] - 1)
+    sender_copy = pltpu.make_async_copy(found, sender, sender_sem)
+    sender_copy.start()
+    senders = held.mesh_sender[...]
+    owner = senders >> 5
+    row = senders & (NODES - 1)
+    rel = ((((owner >> 4) - lat) & (LATS - 1)) << 4) | (((owner & 15) - lon) & (LONS - 1))
+    owner2 = hot((iota((2 * PAIRS, EDGES), 0) >> 1) == rel)
+    row2 = hot((iota((128, EDGES), 0) >> 1) == row)
+    asked = mm_nt(owner2, row2)
+    shape = (2 * PAIRS, 128)
+    same = (iota(shape, 0) & 1) == (iota(shape, 1) & 1)
+    asked = hot((asked > 0.5) & same & (iota(shape, 0) >= 2))
+    req_out[...] = asked.reshape(PAIRS, 2, 128)
+    req_in[0] = jnp.zeros((2, 128), BF)
+    for t in range(STEPS):
+        in_rows[t, 0] = jnp.zeros((2, D), BF)
 
     def ask(step_lat, step_lon):
         i = step_lat * LONS + step_lon

time: 40.8 us -> 40.8 us (level)
  no operation moved by 1% of the time
where the time goes in v9:
time: 40.8 us; the launch traced here: 40.7 us
  Pallas kernels  39.1 us (96%)
  local copies, waits for them, and re-layouts  1.5 us (4%)
    pallas_call x1, Pallas kernels, on_device(): pl.pallas_call(kernel, out_shape=jax.ShapeDtypeStruct((NODES * batch, D),...  39.1 us
    reshape x1, local copies, waits for them, and re-layouts, on_device(): return pl.pallas_call(kernel, out_shape=jax.ShapeDtypeStruct((NODES * bat...  1.5 us

profile of v9, /device:TPU:1, one launch (start us, length us, event | category | flops | bytes accessed | tf_op | source)
XLA Modules:
  0.0 40.7 jit_solution(15874226844312692142)
XLA Ops:
  0.0 39.1 %shard_map.262 = bf16[64,512]{1,0:T(8,128)(2,1)} custom-call(bf16[48,64,2,227]{3,2,1,0:T(2,128)(2,1)} %refs_0_.1, s32[1,128]{1,0:T(1,128)} %bitcast.18, s32[1,128]{1,0:T(1,128)} %bitcast.19, s32[1,256]{1,0:T(1,128)} %bitcast.16, s32[1,256]{1,0:T(1,128)} %bitcast.17, bf16[32,512]{1,0:T(8,128)(2,1)} %refs_5_.1, bf16[128,512]{1,0:T(8,128)(2,1)} %refs_6_.1, ...), custom_call_target="tpu_custom_call" | custom-call | flops 4000000000 | bytes 15000000 | tf_op jit(solution)/shard_map/pallas_call | solution.py:570
  39.2 1.5 %reshape.43 = bf16[32,2,512]{2,1,0:T(2,128)(2,1)} reshape(bf16[64,512]{1,0:T(8,128)(2,1)} %shard_map.262) | data formatting | bytes 131072 | tf_op jit(solution)/shard_map/reshape | solution.py:582

commit v10 on v9

--- a/solution.py
+++ b/solution.py
@@ -356,12 +356,6 @@
 
     lax.fori_loop(0, GRID_EDGES, pick, 0, unroll=32)
 
-    inputs = picked[...].reshape(2 * GRID_EDGES, picked.shape[2])
-    bias = held.embed_b1[...]
-    hidden = by_rows(lambda v: silu(v + bias).astype(BF), mm(inputs, held.embed_w1[...]))
-    gain = held.embed_gain[...]
-    latent = by_rows(lambda v: norm(v, gain).astype(BF), mm(hidden, held.embed_w2[...]))
-    hidden = silu_rows(mm(latent, held.enc_edge_w1[1]), grid_base)
     pltpu.make_async_copy(
         req_in.at[pl.ds(1, PAIRS - 1)], req_in.at[pl.ds(1, PAIRS - 1)], req_recv
     ).wait()
@@ -386,6 +380,12 @@
     pick_all[: 2 * PAIRS] = first
     pick_all[2 * PAIRS :] = more
 
+    inputs = picked[...].reshape(2 * GRID_EDGES, picked.shape[2])
+    bias = held.embed_b1[...]
+    hidden = by_rows(lambda v: silu(v + bias).astype(BF), mm(inputs, held.embed_w1[...]))
+    gain = held.embed_gain[...]
+    latent = by_rows(lambda v: norm(v, gain).astype(BF), mm(hidden, held.embed_w2[...]))
+    hidden = silu_rows(mm(latent, held.enc_edge_w1[1]), grid_base)
     new_edges = updated_rows(grid_edges, mm(hidden, held.enc_edge_w2[...]), held.enc_edge_gain[...])
     summed = mm(total_grid, new_edges).astype(BF)
     hidden = silu(enc_node_base + mm(summed, held.enc_node_w1[1])).astype(BF)
@@ -431,25 +431,21 @@
             far = jnp.where((rank == 0) & (rel > 0), rel, nowhere)
             close = jnp.where(rank == 0, nowhere, 2 * NODES + EXTRA * near + rank - 1)
             close = jnp.where(rel == 0, NODES + row, close)
+            receivers = held.mesh_receiver[...]
+            shape = (2 * EDGES, EDGES)
+            twice = hot(iota(shape, 1) == (iota(shape, 0) >> 1))
+            columns = jnp.concatenate([far, close, receivers, jnp.zeros((5, EDGES), I32)], axis=0)
+            columns = mm_nt(twice, columns.astype(F32).astype(BF)).astype(I32)
             shape = (2 * EDGES, 2 * PAIRS)
-            gather_far[...] = hot(
-                iota(shape, 1) == 2 * doubled_column(far, EDGES) + (iota(shape, 0) & 1)
-            )
-            receivers = held.mesh_receiver[...]
+            gather_far[...] = hot(iota(shape, 1) == 2 * columns[:, 0:1] + (iota(shape, 0) & 1))
             shape = (2 * EDGES, CLOSE)
             lane = iota(shape, 1) - (iota(shape, 0) & 1)
-            gather_close[...] = hot(
-                (lane == 2 * doubled_column(receivers, EDGES))
-                | (lane == 2 * doubled_column(close, EDGES))
-            )
+            gather_close[...] = hot((lane == 2 * columns[:, 2:3]) | (lane == 2 * columns[:, 1:2]))
             shape = (2 * NODES, 2 * EDGES)
             total_mesh = hot(iota(shape, 0) == 2 * doubled_row(receivers, EDGES) + (iota(shape, 1) & 1))
 
             ready(fetch.mesh_edges)
-            shape = (2 * EDGES, EDGES)
-            edge_state = mm(
-                hot(iota(shape, 1) == (iota(shape, 0) >> 1)), held.mesh_edges[...]
-            ).astype(BF)
+            edge_state = mm(twice, held.mesh_edges[...]).astype(BF)
 
         close_rows[: 2 * NODES] = mm(state, held.proc_edge_w1[t, 2]).astype(BF)
         close_rows[2 * NODES : 4 * NODES] = outgoing

time: 40.8 us -> 41.1 us (level)
  no operation moved by 1% of the time
where the time goes in v10:
time: 41.1 us; the launch traced here: 41 us
  Pallas kernels  39.5 us (96%)
  local copies, waits for them, and re-layouts  1.5 us (4%)
    pallas_call x1, Pallas kernels, on_device(): pl.pallas_call(kernel, out_shape=jax.ShapeDtypeStruct((NODES * batch, D),...  39.5 us
    reshape x1, local copies, waits for them, and re-layouts, on_device(): return pl.pallas_call(kernel, out_shape=jax.ShapeDtypeStruct((NODES * bat...  1.5 us

profile of v10, /device:TPU:1, one launch (start us, length us, event | category | flops | bytes accessed | tf_op | source)
XLA Modules:
  0.0 41.0 jit_solution(5166662499578701772)
XLA Ops:
  0.0 39.5 %shard_map.262 = bf16[64,512]{1,0:T(8,128)(2,1)} custom-call(bf16[48,64,2,227]{3,2,1,0:T(2,128)(2,1)} %refs_0_.1, s32[1,128]{1,0:T(1,128)} %bitcast.18, s32[1,128]{1,0:T(1,128)} %bitcast.19, s32[1,256]{1,0:T(1,128)} %bitcast.16, s32[1,256]{1,0:T(1,128)} %bitcast.17, bf16[32,512]{1,0:T(8,128)(2,1)} %refs_5_.1, bf16[128,512]{1,0:T(8,128)(2,1)} %refs_6_.1, ...), custom_call_target="tpu_custom_call" | custom-call | flops 4000000000 | bytes 15000000 | tf_op jit(solution)/shard_map/pallas_call | solution.py:566
  39.5 1.5 %reshape.43 = bf16[32,2,512]{2,1,0:T(2,128)(2,1)} reshape(bf16[64,512]{1,0:T(8,128)(2,1)} %shard_map.262) | data formatting | bytes 131072 | tf_op jit(solution)/shard_map/reshape | solution.py:578

commit v11 on v9

--- a/solution.py
+++ b/solution.py
@@ -92,7 +92,7 @@
 
 
 FETCHED = len(Held._fields)
-FIRST = FETCHED - 9
+BASE = 8
 PIECES = 4
 
 
@@ -270,7 +270,7 @@
         for copy in groups[2]:
             copy.start()
 
-    for copy in fetches[4:FIRST]:
+    for copy in fetches[4:BASE]:
         copy.start()
 
     ready(fetch.g2m_sender, fetch.g2m_receiver, fetch.mesh_sender, fetch.mesh_receiver)
@@ -305,7 +305,7 @@
 
     for_all_others(ask)
 
-    for copy in fetches[FIRST:]:
+    for copy in fetches[BASE:]:
         copy.start()
 
     grid_receivers = held.g2m_receiver[...]
@@ -362,6 +362,8 @@
     gain = held.embed_gain[...]
     latent = by_rows(lambda v: norm(v, gain).astype(BF), mm(hidden, held.embed_w2[...]))
     hidden = silu_rows(mm(latent, held.enc_edge_w1[1]), grid_base)
+    new_edges = updated_rows(grid_edges, mm(hidden, held.enc_edge_w2[...]), held.enc_edge_gain[...])
+    summed = mm(total_grid, new_edges).astype(BF)
     pltpu.make_async_copy(
         req_in.at[pl.ds(1, PAIRS - 1)], req_in.at[pl.ds(1, PAIRS - 1)], req_recv
     ).wait()
@@ -386,8 +388,6 @@
     pick_all[: 2 * PAIRS] = first
     pick_all[2 * PAIRS :] = more
 
-    new_edges = updated_rows(grid_edges, mm(hidden, held.enc_edge_w2[...]), held.enc_edge_gain[...])
-    summed = mm(total_grid, new_edges).astype(BF)
     hidden = silu(enc_node_base + mm(summed, held.enc_node_w1[1])).astype(BF)
     update = norm(mm(hidden, held.enc_node_w2[...]), held.enc_node_gain[...])
     state = (state.astype(F32) + update).astype(BF)

time: 40.8 us -> 40.8 us (level)
  no operation moved by 1% of the time
where the time goes in v11:
time: 40.8 us; the launch traced here: 40.6 us
  Pallas kernels  39.1 us (96%)
  local copies, waits for them, and re-layouts  1.5 us (4%)
    pallas_call x1, Pallas kernels, on_device(): pl.pallas_call(kernel, out_shape=jax.ShapeDtypeStruct((NODES * batch, D),...  39.1 us
    reshape x1, local copies, waits for them, and re-layouts, on_device(): return pl.pallas_call(kernel, out_shape=jax.ShapeDtypeStruct((NODES * bat...  1.5 us

profile of v11, /device:TPU:1, one launch (start us, length us, event | category | flops | bytes accessed | tf_op | source)
XLA Modules:
  0.0 40.6 jit_solution(2689054206365306498)
XLA Ops:
  0.0 39.1 %shard_map.262 = bf16[64,512]{1,0:T(8,128)(2,1)} custom-call(bf16[48,64,2,227]{3,2,1,0:T(2,128)(2,1)} %refs_0_.1, s32[1,128]{1,0:T(1,128)} %bitcast.18, s32[1,128]{1,0:T(1,128)} %bitcast.19, s32[1,256]{1,0:T(1,128)} %bitcast.16, s32[1,256]{1,0:T(1,128)} %bitcast.17, bf16[32,512]{1,0:T(8,128)(2,1)} %refs_5_.1, bf16[128,512]{1,0:T(8,128)(2,1)} %refs_6_.1, ...), custom_call_target="tpu_custom_call" | custom-call | flops 4000000000 | bytes 15000000 | tf_op jit(solution)/shard_map/pallas_call | solution.py:570
  39.1 1.5 %reshape.43 = bf16[32,2,512]{2,1,0:T(2,128)(2,1)} reshape(bf16[64,512]{1,0:T(8,128)(2,1)} %shard_map.262) | data formatting | bytes 131072 | tf_op jit(solution)/shard_map/reshape | solution.py:582

commit v12 on v11

--- a/solution.py
+++ b/solution.py
@@ -157,11 +157,11 @@
     refs = refs[2 + FETCHED :]
     held = Held(*refs[:FETCHED])
     (
-        cells, found, sender, picked, pick_all, gather_far, gather_close, close_rows, edge_base,
+        cells, found, sender, picked, asked_row, asked_place, own_rows, gather_far, gather_close, close_rows, edge_base,
         req_out, req_in, out_rows, in_rows,
         fetch_sem, cells_sem, sender_sem,
         halo_send, halo_recv, req_send, req_recv, row_send, row_recv,
-        more_send, more_recv,
+        more_send, more_recv, asked_sem,
     ) = refs[FETCHED:]
 
     lat = lax.axis_index("lat")
@@ -362,8 +362,6 @@
     gain = held.embed_gain[...]
     latent = by_rows(lambda v: norm(v, gain).astype(BF), mm(hidden, held.embed_w2[...]))
     hidden = silu_rows(mm(latent, held.enc_edge_w1[1]), grid_base)
-    new_edges = updated_rows(grid_edges, mm(hidden, held.enc_edge_w2[...]), held.enc_edge_gain[...])
-    summed = mm(total_grid, new_edges).astype(BF)
     pltpu.make_async_copy(
         req_in.at[pl.ds(1, PAIRS - 1)], req_in.at[pl.ds(1, PAIRS - 1)], req_recv
     ).wait()
@@ -385,18 +383,29 @@
     choose = hot(iota(shape, 1) == 2 * target + (line & 1))
     kth = ((line >> 1) - EXTRA * which + 1).astype(F32)[:, : 2 * NODES]
     more = jnp.where(mm(choose, place_of) == kth, mm(choose, wanted), 0.0).astype(BF)
-    pick_all[: 2 * PAIRS] = first
-    pick_all[2 * PAIRS :] = more
-
+    lanes = iota((8, 2 * NODES), 1).astype(F32).astype(BF)
+    chosen = mm_nt(lanes, jnp.concatenate([first, more], axis=0)).astype(I32)
+    asked_row[...] = (chosen[0:1] >> 1) & (NODES - 1)
+    asked_copy = pltpu.make_async_copy(asked_row, asked_place, asked_sem)
+    asked_copy.start()
+
+    new_edges = updated_rows(grid_edges, mm(hidden, held.enc_edge_w2[...]), held.enc_edge_gain[...])
+    summed = mm(total_grid, new_edges).astype(BF)
     hidden = silu(enc_node_base + mm(summed, held.enc_node_w1[1])).astype(BF)
     update = norm(mm(hidden, held.enc_node_w2[...]), held.enc_node_gain[...])
     state = (state.astype(F32) + update).astype(BF)
 
     ready(fetch.proc_edge_w1)
+    asked_copy.wait()
     for t in range(STEPS):
         outgoing = mm(state, held.proc_edge_w1[t, 1]).astype(BF)
-        out_rows[t] = mm(pick_all[...], outgoing).astype(BF).reshape(SLOTS, 2, D)
-
+        own_rows[...] = outgoing.reshape(NODES, 2, D)
+
+        def fill(i, t=t):
+            out_rows[t, i] = own_rows[asked_place[0, 2 * i]]
+
+        for i in range(PAIRS, SLOTS):
+            fill(i)
         for n, i in enumerate(NEAR):
             span = pl.ds(PAIRS + EXTRA * n, EXTRA)
             pltpu.make_async_remote_copy(
@@ -413,7 +422,19 @@
                 device_id=place(step_lat, step_lon, -1), device_id_type=MESH,
             ).start()
 
-        for_all_others(give)
+        for step_lon in range(1, LONS):
+            fill(step_lon)
+        for step_lon in range(1, LONS):
+            give(0, step_lon)
+
+        def give_band(step_lat, carry, fill=fill, give=give):
+            for step_lon in range(LONS):
+                fill(step_lat * LONS + step_lon)
+            for step_lon in range(LONS):
+                give(step_lat, step_lon)
+            return carry
+
+        lax.fori_loop(1, LATS, give_band, 0)
 
         if t == 0:
             ready(fetch.proc_edge_b1, fetch.proc_edge_w2, fetch.proc_edge_gain)
@@ -546,7 +567,9 @@
         pltpu.VMEM((2, GRID_EDGES), I32),
         pltpu.SMEM((2, GRID_EDGES), I32),
         pltpu.VMEM((GRID_EDGES, batch, width), BF),
-        pltpu.VMEM((2 * SLOTS, 2 * NODES), BF),
+        pltpu.VMEM((1, 2 * SLOTS), I32),
+        pltpu.SMEM((1, 2 * SLOTS), I32),
+        pltpu.VMEM((NODES, 2, D), BF),
         pltpu.VMEM((2 * EDGES, 2 * PAIRS), BF),
         pltpu.VMEM((2 * EDGES, CLOSE), BF),
         pltpu.VMEM((CLOSE, D), BF),
@@ -566,6 +589,7 @@
         dma((STEPS,)),
         dma((STEPS,)),
         dma((STEPS,)),
+        dma,
     ]
     return pl.pallas_call(
         kernel,

time: 40.8 us -> 40.7 us (level)
  no operation moved by 1% of the time
where the time goes in v12:
time: 40.7 us; the launch traced here: 40.5 us
  Pallas kernels  39 us (96%)
  local copies, waits for them, and re-layouts  1.5 us (4%)
    pallas_call x1, Pallas kernels, on_device(): pl.pallas_call(kernel, out_shape=jax.ShapeDtypeStruct((NODES * batch, D),...  39 us
    reshape x1, local copies, waits for them, and re-layouts, on_device(): return pl.pallas_call(kernel, out_shape=jax.ShapeDtypeStruct((NODES * bat...  1.5 us

profile of v12, /device:TPU:1, one launch (start us, length us, event | category | flops | bytes accessed | tf_op | source)
XLA Modules:
  0.0 40.5 jit_solution(5099094284205375058)
XLA Ops:
  0.0 39.0 %shard_map.262 = bf16[64,512]{1,0:T(8,128)(2,1)} custom-call(bf16[48,64,2,227]{3,2,1,0:T(2,128)(2,1)} %refs_0_.1, s32[1,128]{1,0:T(1,128)} %bitcast.18, s32[1,128]{1,0:T(1,128)} %bitcast.19, s32[1,256]{1,0:T(1,128)} %bitcast.16, s32[1,256]{1,0:T(1,128)} %bitcast.17, bf16[32,512]{1,0:T(8,128)(2,1)} %refs_5_.1, bf16[128,512]{1,0:T(8,128)(2,1)} %refs_6_.1, ...), custom_call_target="tpu_custom_call" | custom-call | flops 4000000000 | bytes 15000000 | tf_op jit(solution)/shard_map/pallas_call | solution.py:594
  39.0 1.5 %reshape.43 = bf16[32,2,512]{2,1,0:T(2,128)(2,1)} reshape(bf16[64,512]{1,0:T(8,128)(2,1)} %shard_map.262) | data formatting | bytes 131072 | tf_op jit(solution)/shard_map/reshape | solution.py:606

commit v13 on v12

--- a/solution.py
+++ b/solution.py
@@ -452,25 +452,21 @@
             far = jnp.where((rank == 0) & (rel > 0), rel, nowhere)
             close = jnp.where(rank == 0, nowhere, 2 * NODES + EXTRA * near + rank - 1)
             close = jnp.where(rel == 0, NODES + row, close)
+            receivers = held.mesh_receiver[...]
+            shape = (2 * EDGES, EDGES)
+            twice = hot(iota(shape, 1) == (iota(shape, 0) >> 1))
+            columns = jnp.concatenate([far, close, receivers, jnp.zeros((5, EDGES), I32)], axis=0)
+            columns = mm_nt(twice, columns.astype(F32).astype(BF)).astype(I32)
             shape = (2 * EDGES, 2 * PAIRS)
-            gather_far[...] = hot(
-                iota(shape, 1) == 2 * doubled_column(far, EDGES) + (iota(shape, 0) & 1)
-            )
-            receivers = held.mesh_receiver[...]
+            gather_far[...] = hot(iota(shape, 1) == 2 * columns[:, 0:1] + (iota(shape, 0) & 1))
             shape = (2 * EDGES, CLOSE)
             lane = iota(shape, 1) - (iota(shape, 0) & 1)
-            gather_close[...] = hot(
-                (lane == 2 * doubled_column(receivers, EDGES))
-                | (lane == 2 * doubled_column(close, EDGES))
-            )
+            gather_close[...] = hot((lane == 2 * columns[:, 2:3]) | (lane == 2 * columns[:, 1:2]))
             shape = (2 * NODES, 2 * EDGES)
             total_mesh = hot(iota(shape, 0) == 2 * doubled_row(receivers, EDGES) + (iota(shape, 1) & 1))
 
             ready(fetch.mesh_edges)
-            shape = (2 * EDGES, EDGES)
-            edge_state = mm(
-                hot(iota(shape, 1) == (iota(shape, 0) >> 1)), held.mesh_edges[...]
-            ).astype(BF)
+            edge_state = mm(twice, held.mesh_edges[...]).astype(BF)
 
         close_rows[: 2 * NODES] = mm(state, held.proc_edge_w1[t, 2]).astype(BF)
         close_rows[2 * NODES : 4 * NODES] = outgoing
@@ -484,6 +480,26 @@
             + held.proc_edge_b1[t : t + 1]
         )
 
+        if t == 0:
+            for copy in groups[0]:
+                copy.wait_send()
+
+            @pl.when(has_before)
+            def _():
+                for copy in groups[1]:
+                    copy.wait_send()
+
+            @pl.when(has_after)
+            def _():
+                for copy in groups[2]:
+                    copy.wait_send()
+
+            asked_all = req_out.at[pl.ds(1, PAIRS - 1)]
+            pltpu.make_async_copy(asked_all, asked_all, req_send).wait()
+        sent = out_rows.at[t, pl.ds(PAIRS, SLOTS - PAIRS)]
+        pltpu.make_async_copy(sent, sent, more_send.at[t]).wait()
+        sent = out_rows.at[t, pl.ds(1, PAIRS - 1)]
+        pltpu.make_async_copy(sent, sent, row_send.at[t]).wait()
         arrived = in_rows.at[t, pl.ds(1, PAIRS - 1)]
         pltpu.make_async_copy(arrived, arrived, row_recv.at[t]).wait()
         table = in_rows[t, :PAIRS].reshape(2 * PAIRS, D)
@@ -500,27 +516,6 @@
         state = (state.astype(F32) + update).astype(BF)
 
     out_ref[...] = state
-
-    for copy in groups[0]:
-        copy.wait_send()
-
-    @pl.when(has_before)
-    def _():
-        for copy in groups[1]:
-            copy.wait_send()
-
-    @pl.when(has_after)
-    def _():
-        for copy in groups[2]:
-            copy.wait_send()
-
-    asked_all = req_out.at[pl.ds(1, PAIRS - 1)]
-    pltpu.make_async_copy(asked_all, asked_all, req_send).wait()
-    for t in range(STEPS):
-        sent = out_rows.at[t, pl.ds(1, PAIRS - 1)]
-        pltpu.make_async_copy(sent, sent, row_send.at[t]).wait()
-        sent = out_rows.at[t, pl.ds(PAIRS, SLOTS - PAIRS)]
-        pltpu.make_async_copy(sent, sent, more_send.at[t]).wait()
 
 
 def on_device(*args):

time: 40.7 us -> 40.7 us (level)
  no operation moved by 1% of the time
where the time goes in v13:
time: 40.7 us; the launch traced here: 40.5 us
  Pallas kernels  39 us (96%)
  local copies, waits for them, and re-layouts  1.5 us (4%)
    pallas_call x1, Pallas kernels, on_device(): pl.pallas_call(kernel, out_shape=jax.ShapeDtypeStruct((NODES * batch, D),...  39 us
    reshape x1, local copies, waits for them, and re-layouts, on_device(): return pl.pallas_call(kernel, out_shape=jax.ShapeDtypeStruct((NODES * bat...  1.5 us

profile of v13, /device:TPU:1, one launch (start us, length us, event | category | flops | bytes accessed | tf_op | source)
XLA Modules:
  0.0 40.5 jit_solution(885243996915956555)
XLA Ops:
  0.0 39.0 %shard_map.262 = bf16[64,512]{1,0:T(8,128)(2,1)} custom-call(bf16[48,64,2,227]{3,2,1,0:T(2,128)(2,1)} %refs_0_.1, s32[1,128]{1,0:T(1,128)} %bitcast.18, s32[1,128]{1,0:T(1,128)} %bitcast.19, s32[1,256]{1,0:T(1,128)} %bitcast.16, s32[1,256]{1,0:T(1,128)} %bitcast.17, bf16[32,512]{1,0:T(8,128)(2,1)} %refs_5_.1, bf16[128,512]{1,0:T(8,128)(2,1)} %refs_6_.1, ...), custom_call_target="tpu_custom_call" | custom-call | flops 4000000000 | bytes 15000000 | tf_op jit(solution)/shard_map/pallas_call | solution.py:589
  39.0 1.5 %reshape.43 = bf16[32,2,512]{2,1,0:T(2,128)(2,1)} reshape(bf16[64,512]{1,0:T(8,128)(2,1)} %shard_map.262) | data formatting | bytes 131072 | tf_op jit(solution)/shard_map/reshape | solution.py:601

commit v14 on v13

--- a/solution.py
+++ b/solution.py
@@ -504,13 +504,9 @@
         pltpu.make_async_copy(arrived, arrived, row_recv.at[t]).wait()
         table = in_rows[t, :PAIRS].reshape(2 * PAIRS, D)
         gain = held.proc_edge_gain[t : t + 1]
-        halves = []
-        for span in (slice(0, EDGES), slice(EDGES, 2 * EDGES)):
-            hidden = silu_rows(mm(gather_far[span], table), edge_base[span])
-            halves.append(updated_rows(edge_state[span], mm(hidden, held.proc_edge_w2[t]), gain))
-        edge_state = jnp.concatenate(halves, axis=0)
-        summed = mm(total_mesh[:, :EDGES], halves[0]) + mm(total_mesh[:, EDGES:], halves[1])
-        summed = summed.astype(BF)
+        hidden = silu_rows(mm(gather_far[...], table), edge_base)
+        edge_state = updated_rows(edge_state, mm(hidden, held.proc_edge_w2[t]), gain)
+        summed = mm(total_mesh, edge_state).astype(BF)
         hidden = silu(node_base + mm(summed, held.proc_node_w1[t, 1])).astype(BF)
         update = norm(mm(hidden, held.proc_node_w2[t]), held.proc_node_gain[t : t + 1])
         state = (state.astype(F32) + update).astype(BF)

time: 40.7 us -> 40.5 us (level)
  no operation moved by 1% of the time
where the time goes in v14:
time: 40.5 us; the launch traced here: 40.4 us
  Pallas kernels  38.9 us (96%)
  local copies, waits for them, and re-layouts  1.5 us (4%)
    pallas_call x1, Pallas kernels, on_device(): pl.pallas_call(kernel, out_shape=jax.ShapeDtypeStruct((NODES * batch, D),...  38.9 us
    reshape x1, local copies, waits for them, and re-layouts, on_device(): return pl.pallas_call(kernel, out_shape=jax.ShapeDtypeStruct((NODES * bat...  1.5 us

profile of v14, /device:TPU:1, one launch (start us, length us, event | category | flops | bytes accessed | tf_op | source)
XLA Modules:
  0.0 40.4 jit_solution(6886371033265451123)
XLA Ops:
  0.0 38.9 %shard_map.262 = bf16[64,512]{1,0:T(8,128)(2,1)} custom-call(bf16[48,64,2,227]{3,2,1,0:T(2,128)(2,1)} %refs_0_.1, s32[1,128]{1,0:T(1,128)} %bitcast.18, s32[1,128]{1,0:T(1,128)} %bitcast.19, s32[1,256]{1,0:T(1,128)} %bitcast.16, s32[1,256]{1,0:T(1,128)} %bitcast.17, bf16[32,512]{1,0:T(8,128)(2,1)} %refs_5_.1, bf16[128,512]{1,0:T(8,128)(2,1)} %refs_6_.1, ...), custom_call_target="tpu_custom_call" | custom-call | flops 4000000000 | bytes 15000000 | tf_op jit(solution)/shard_map/pallas_call | solution.py:585
  38.9 1.5 %reshape.43 = bf16[32,2,512]{2,1,0:T(2,128)(2,1)} reshape(bf16[64,512]{1,0:T(8,128)(2,1)} %shard_map.262) | data formatting | bytes 131072 | tf_op jit(solution)/shard_map/reshape | solution.py:597

commit v15 on v14

--- a/solution.py
+++ b/solution.py
@@ -16,7 +16,7 @@
 D = 512
 HALO = 2
 STEPS = 2
-CHUNK = 64
+CHUNK = 128
 LATS = 8
 LONS = 16
 PAIRS = LATS * LONS

time: 40.5 us -> 40.5 us (level)
  no operation moved by 1% of the time
where the time goes in v15:
time: 40.5 us; the launch traced here: 40.4 us
  Pallas kernels  38.9 us (96%)
  local copies, waits for them, and re-layouts  1.5 us (4%)
    pallas_call x1, Pallas kernels, on_device(): pl.pallas_call(kernel, out_shape=jax.ShapeDtypeStruct((NODES * batch, D),...  38.9 us
    reshape x1, local copies, waits for them, and re-layouts, on_device(): return pl.pallas_call(kernel, out_shape=jax.ShapeDtypeStruct((NODES * bat...  1.5 us

profile of v15, /device:TPU:1, one launch (start us, length us, event | category | flops | bytes accessed | tf_op | source)
XLA Modules:
  0.0 40.4 jit_solution(6886371033265451123)
XLA Ops:
  0.0 38.9 %shard_map.262 = bf16[64,512]{1,0:T(8,128)(2,1)} custom-call(bf16[48,64,2,227]{3,2,1,0:T(2,128)(2,1)} %refs_0_.1, s32[1,128]{1,0:T(1,128)} %bitcast.18, s32[1,128]{1,0:T(1,128)} %bitcast.19, s32[1,256]{1,0:T(1,128)} %bitcast.16, s32[1,256]{1,0:T(1,128)} %bitcast.17, bf16[32,512]{1,0:T(8,128)(2,1)} %refs_5_.1, bf16[128,512]{1,0:T(8,128)(2,1)} %refs_6_.1, ...), custom_call_target="tpu_custom_call" | custom-call | flops 4000000000 | bytes 15000000 | tf_op jit(solution)/shard_map/pallas_call | solution.py:585
  38.9 1.5 %reshape.43 = bf16[32,2,512]{2,1,0:T(2,128)(2,1)} reshape(bf16[64,512]{1,0:T(8,128)(2,1)} %shard_map.262) | data formatting | bytes 131072 | tf_op jit(solution)/shard_map/reshape | solution.py:597
